TPU v7x, 32 devices: a whole 2x2x4 slice. The times are simulated.
32 devices in a mesh: head: 2 (over y), blk: 16 (over z, x, core).
Axes of the slice: x: 2, y: 2, z: 4, core: 2. Of those that a mesh axis runs over, the one named last changes fastest.
Arguments:
- tokens: bfloat16 [4096, 1536], P(('head', 'blk')), may hold values from -6 to 6
- cotangent: bfloat16 [4096, 1536], P(('head', 'blk')), may hold values from -6 to 6
- seq_lengths: int32 [3], replicated, may hold values from 1 to 2048, 4096 in all
- piece_order: int32 [32], replicated, may hold values from 0 to 31, each once
- routes: int32 [4096, 6], P(('head', 'blk')), may hold values from 0 to 15, all different within a row; in each aligned block of 128 rows (0 to 127, 128 to 255, ...) at most 64 rows name the same one
- norm1_gain: bfloat16 [1536], P(('head', 'blk')), may hold values from 0.5 to 1.5
- w_query: bfloat16 [1536, 1536], P(('head', 'blk')), may hold values from -0.15625 to 0.15625
- w_key: bfloat16 [1536, 512], P(('head', 'blk')), may hold values from -0.15625 to 0.15625
- w_value: bfloat16 [1536, 512], P(('head', 'blk')), may hold values from -0.15625 to 0.15625
- w_out: bfloat16 [1536, 1536], P(('head', 'blk')), may hold values from -1.75 to 1.75
- norm2_gain: bfloat16 [1536], P(('head', 'blk')), may hold values from 0.5 to 1.5
- w_router: bfloat16 [1536, 16], P(('head', 'blk')), may hold values from -0.078125 to 0.078125
- shared_up: bfloat16 [1536, 2048], P(('head', 'blk')), may hold values from -0.15625 to 0.15625
- shared_down: bfloat16 [1024, 1536], P(('head', 'blk')), may hold values from -0.1875 to 0.1875
- expert_up: bfloat16 [16, 1536, 1024], P('blk', 'head'), may hold values from -0.15625 to 0.15625
- expert_down: bfloat16 [16, 512, 1536], P('blk', None, 'head'), may hold values from -0.25 to 0.25
Outputs:
- output: bfloat16 [4096, 1536], P(('head', 'blk'))
- input_grad: float32 [4096, 1536], P(('head', 'blk'))
- norm1_gain_grad: float32 [1536], P(('head', 'blk'))
- w_query_grad: float32 [1536, 1536], P(('head', 'blk'))
- w_key_grad: float32 [1536, 512], P(('head', 'blk'))
- w_value_grad: float32 [1536, 512], P(('head', 'blk'))
- w_out_grad: float32 [1536, 1536], P(('head', 'blk'))
- norm2_gain_grad: float32 [1536], P(('head', 'blk'))
- w_router_grad: float32 [1536, 16], P(('head', 'blk'))
- shared_up_grad: float32 [1536, 2048], P(('head', 'blk'))
- shared_down_grad: float32 [1024, 1536], P(('head', 'blk'))
- expert_up_grad: float32 [16, 1536, 1024], P('blk', 'head')
- expert_down_grad: float32 [16, 512, 1536], P('blk', None, 'head')
Inputs may be any that keep to these rules, and one draw needn't show every extreme that they name: `routes`: every row names 6 different experts. Among the 128 rows of one device no expert is named more than 64 times; in every draw some device names some expert exactly 64 times. `seq_lengths`: the lengths sum to 4096; the largest is exactly 2048. Each number appears once: dealt piece p holds the stream positions piece_order[p] * 128 to piece_order[p] * 128 + 127.
All inputs are finite; a program needn't handle non-finite values.
Results may differ from a plain program's by a relative error of at most 0.025.
Values may be sent and summed in bfloat16 or wider, within the bound.
A program may use at most 256 MiB of HBM per device.

v0:
```python
import functools

import jax
import jax.numpy as jnp
from jax import lax
from jax.experimental import pallas as pl
from jax.experimental.pallas import tpu as pltpu
from jax.sharding import PartitionSpec as P

MESH = pl.DeviceIdType.MESH


def ring_place(chip, chips):
    odd = chip % 2
    return (chip // 2) * (1 - odd) + (chips - 1 - chip // 2) * odd


def ring_chip(place, chips):
    high = place // (chips // 2)
    return 2 * place * (1 - high) + (2 * (chips - 1 - place) + 1) * high


def ring_info(chips):
    blk = lax.axis_index("blk")
    chip, core = blk // 2, blk % 2
    place = ring_place(chip, chips)

    def at(step):
        return ring_chip((place + step + chips) % chips, chips) * 2 + core

    return blk, core, at, blk + 1 - 2 * core


def pieces_of(shape):
    if len(shape) == 3:
        return [(0, None), (1, None)]
    rows = shape[0]
    if rows >= 32 and rows % 16 == 0:
        cut = (rows // 2 + 15) // 16 * 16
        return [(0, cut), (cut, rows - cut)]
    return [(0, rows)]


def part_in(ref, piece):
    start, size = piece
    return ref.at[start] if size is None else ref.at[pl.ds(start, size)]


def part_out(ref, piece, b):
    start, size = piece
    return ref.at[start, b] if size is None else ref.at[b, pl.ds(start, size)]


def ag_kernel(count, chips, plans, *refs):
    ins, outs = refs[:count], refs[count : 2 * count]
    right_sem, left_sem, sib_sem, sright, sleft, ssib, own_sem = refs[2 * count :]
    blk, core, at, sib = ring_info(chips)
    right, left = at(1), at(-1)
    barrier = pltpu.get_barrier_semaphore()
    for other in (right, left, sib):
        pl.semaphore_signal(barrier, inc=1, device_id={"blk": other}, device_id_type=MESH)
    pl.semaphore_wait(barrier, 3)
    half = chips // 2
    started = []

    def send(src, dst, ssem, rsem, dev):
        copy = pltpu.make_async_remote_copy(
            src_ref=src, dst_ref=dst, send_sem=ssem, recv_sem=rsem,
            device_id={"blk": dev}, device_id_type=MESH)
        copy.start()
        started.append(copy)
        return copy

    chunks = []
    for k in range(count):
        for i, piece in enumerate(plans[k]):
            chunks.append((len(chunks), k, piece, half - (i % 2), half - 1 + (i % 2)))
    copies = {}
    locals_ = []
    for c, k, piece, rh, lh in chunks:
        src = part_in(ins[k], piece)
        dst = part_out(outs[k], piece, blk)
        if rh >= 1:
            copies[c, "r", 1] = send(src, dst, sright.at[c, 0], right_sem.at[c, 0], right)
        if lh >= 1:
            copies[c, "l", 1] = send(src, dst, sleft.at[c, 0], left_sem.at[c, 0], left)
        copies[c, "s", 0] = send(src, dst, ssib.at[c, 0], sib_sem.at[c, 0], sib)
        own = pltpu.make_async_copy(src, dst, own_sem.at[c])
        own.start()
        locals_.append(own)
    for s in range(1, half + 1):
        for c, k, piece, rh, lh in chunks:
            if s <= rh:
                copies[c, "r", s].wait_recv()
                b = at(-s)
                blockref = part_out(outs[k], piece, b)
                if s < rh:
                    copies[c, "r", s + 1] = send(blockref, blockref, sright.at[c, s], right_sem.at[c, s], right)
                copies[c, "sr", s] = send(blockref, blockref, ssib.at[c, s], sib_sem.at[c, s], sib)
            if s <= lh:
                copies[c, "l", s].wait_recv()
                b = at(s)
                blockref = part_out(outs[k], piece, b)
                if s < lh:
                    copies[c, "l", s + 1] = send(blockref, blockref, sleft.at[c, s], left_sem.at[c, s], left)
                copies[c, "sl", s] = send(blockref, blockref, ssib.at[c, half + s], sib_sem.at[c, half + s], sib)
    for (c, d, s), copy in copies.items():
        if d in ("s", "sr", "sl"):
            copy.wait_recv()
    for copy in started:
        copy.wait_send()
    for copy in locals_:
        copy.wait()


def all_gather_blk(arrays, blks, collective_id, vmem=False):
    chips = blks // 2
    count = len(arrays)
    plans = [pieces_of(a.shape) for a in arrays]
    n = sum(len(p) for p in plans)
    half = chips // 2
    shapes = [
        jax.ShapeDtypeStruct((a.shape[0], blks) + a.shape[1:] if a.ndim == 3 else (blks,) + a.shape, a.dtype)
        for a in arrays
    ]
    dma = pltpu.SemaphoreType.DMA
    space = pltpu.VMEM if vmem else pl.ANY
    return pl.pallas_call(
        functools.partial(ag_kernel, count, chips, plans),
        out_shape=shapes,
        in_specs=[pl.BlockSpec(memory_space=space)] * count,
        out_specs=[pl.BlockSpec(memory_space=space)] * count,
        scratch_shapes=[
            dma((n, half)), dma((n, half)), dma((n, 2 * half + 1)),
            dma((n, half)), dma((n, half)), dma((n, 2 * half + 1)), dma((n,)),
        ],
        compiler_params=pltpu.CompilerParams(collective_id=collective_id, has_side_effects=True,
            vmem_limit_bytes=(60 << 20) if vmem else None),
    )(*arrays)


def rs_kernel(count, chips, plans, *refs):
    xs, outs = refs[:count], refs[count : 2 * count]
    rest = refs[2 * count :]
    n = sum(len(p) for p in plans)
    ys, rs, ls = rest[:n], rest[n : 2 * n], rest[2 * n : 3 * n]
    right_sem, left_sem, sib_sem, sright, sleft, ssib = rest[3 * n :]
    blk, core, at, sib = ring_info(chips)
    right, left = at(1), at(-1)
    barrier = pltpu.get_barrier_semaphore()
    for other in (right, left, sib):
        pl.semaphore_signal(barrier, inc=1, device_id={"blk": other}, device_id_type=MESH)
    pl.semaphore_wait(barrier, 3)
    half = chips // 2
    started = []

    def send(src, dst, ssem, rsem, dev):
        copy = pltpu.make_async_remote_copy(
            src_ref=src, dst_ref=dst, send_sem=ssem, recv_sem=rsem,
            device_id={"blk": dev}, device_id_type=MESH)
        copy.start()
        started.append(copy)
        return copy

    chunks = []
    for k in range(count):
        for i, piece in enumerate(plans[k]):
            chunks.append((len(chunks), k, piece, half - (i % 2), half - 1 + (i % 2)))
    order = []
    for d in range(half, 0, -1):
        order += [d, -d] if d < half else [d]
    order.append(0)
    sibs = {}
    for j, d in enumerate(order):
        there = at(d) + 1 - 2 * core
        for c, k, piece, rh, lh in chunks:
            sibs[c, d] = send(part_out(xs[k], piece, there), ys[c].at[j], ssib.at[c, j], sib_sem.at[c, j], sib)
    ready = set()

    def blocks(rows, body):
        step = 16 if rows % 16 == 0 else rows

        @pl.loop(0, rows // step)
        def _(i):
            body(pl.ds(pl.multiple_of(i * step, step), step))

    def mine(c, k, piece, d):
        j = order.index(d)
        if (c, d) not in ready:
            sibs[c, d].wait_recv()
            ready.add((c, d))
        return j

    copies = {}

    def join(c, k, piece, d, into, recv):
        j = mine(c, k, piece, d)
        x = part_out(xs[k], piece, at(d))
        rows = x.shape[0]

        def body(w):
            total = x[w].astype(jnp.float32) + ys[c][j, w].astype(jnp.float32)
            if recv is not None:
                total = total + recv[w].astype(jnp.float32)
            into[w] = total.astype(into.dtype)

        blocks(rows, body)

    for s in range(1, half + 1):
        for c, k, piece, rh, lh in chunks:
            for way, hops, buf, sem, ssem, dev in (
                (1, rh, rs[c], right_sem, sright, right),
                (-1, lh, ls[c], left_sem, sleft, left),
            ):
                if s > hops:
                    continue
                if s == 1:
                    j = order.index(way * hops if way * hops in order else hops)
                    join(c, k, piece, order[j], ys[c].at[j], None)
                    src = ys[c].at[j]
                else:
                    copies[c, way, s - 1].wait_recv()
                    d = way * (hops - s + 1)
                    src = buf.at[s - 2]
                    join(c, k, piece, d, src, src)
                copies[c, way, s] = send(src, buf.at[s - 1], ssem.at[c, s - 1], sem.at[c, s - 1], dev)
    for c, k, piece, rh, lh in chunks:
        if rh >= 1:
            copies[c, 1, rh].wait_recv()
        if lh >= 1:
            copies[c, -1, lh].wait_recv()
        j = mine(c, k, piece, 0)
        x = part_out(xs[k], piece, blk)
        target = part_in(outs[k], piece)

        def body(w, x=x, c=c, j=j, rh=rh, lh=lh, target=target):
            total = x[w].astype(jnp.float32) + ys[c][j, w].astype(jnp.float32)
            if rh >= 1:
                total = total + rs[c][rh - 1, w].astype(jnp.float32)
            if lh >= 1:
                total = total + ls[c][lh - 1, w].astype(jnp.float32)
            target[w] = total.astype(target.dtype)

        blocks(x.shape[0], body)
    for copy in started:
        copy.wait_send()


def reduce_scatter_blk(arrays, blks, collective_id, out_dtypes):
    chips = blks // 2
    half = chips // 2
    count = len(arrays)
    shapes = [a.shape[1:] if a.ndim == 3 else (2,) + a.shape[2:] for a in arrays]
    plans = [pieces_of(s) for s in shapes]
    dma = pltpu.SemaphoreType.DMA
    ys, rs = [], []
    for s, plan in zip(shapes, plans):
        for start, size in plan:
            rows = s[1] if size is None else size
            ys.append(pltpu.VMEM((chips, rows, s[-1]), jnp.bfloat16))
            rs.append(pltpu.VMEM((half, rows, s[-1]), jnp.bfloat16))
    n = len(ys)
    return pl.pallas_call(
        functools.partial(rs_kernel, count, chips, plans),
        out_shape=[jax.ShapeDtypeStruct(s, t) for s, t in zip(shapes, out_dtypes)],
        in_specs=[pl.BlockSpec(memory_space=pltpu.VMEM)] * count,
        out_specs=[pl.BlockSpec(memory_space=pltpu.VMEM)] * count,
        scratch_shapes=ys + rs + rs + [
            dma((n, half)), dma((n, half)), dma((n, chips)),
            dma((n, half)), dma((n, half)), dma((n, chips)),
        ],
        compiler_params=pltpu.CompilerParams(collective_id=collective_id, has_side_effects=True,
            vmem_limit_bytes=60 << 20),
    )(*arrays)


H = 12
KVH = 4
HD = 128
TOP = 6
PIECE = 128
EPS = 1e-05
NEG = -1e30
F32 = jnp.float32
BF16 = jnp.bfloat16


def dot(a, b):
    return jnp.dot(a, b, preferred_element_type=F32)


def dot_first(a, b):
    return lax.dot_general(a, b, (((0,), (0,)), ((), ())), preferred_element_type=F32)


def dot_last(a, b):
    return lax.dot_general(a, b, (((1,), (1,)), ((), ())), preferred_element_type=F32)


def inv_scale(values):
    return lax.rsqrt(jnp.mean(values * values, axis=1, keepdims=True) + EPS)


def norm_back(values, scaler, gain, upstream):
    normed = values * scaler
    gain_grad = jnp.sum(upstream * normed, axis=0)
    scaled = upstream * gain
    grad = scaler * (scaled - normed * jnp.mean(scaled * normed, axis=1, keepdims=True))
    return grad, gain_grad


def gated_grad(act_grad, gate, lift):
    sig = jax.nn.sigmoid(gate)
    return jnp.concatenate(
        [act_grad * lift * sig * (1.0 + gate * (1.0 - sig)), act_grad * gate * sig], axis=1
    ).astype(BF16)


def swap(array):
    return lax.ppermute(array, "head", [(0, 1), (1, 0)])


def ends_of(lengths_ref):
    end, ends = jnp.int32(0), []
    for e in range(lengths_ref.shape[0]):
        end = end + lengths_ref[e]
        ends.append(end)
    return ends


def key_span(place, lengths_ref):
    start = jnp.int32(0)
    for end in ends_of(lengths_ref):
        start = jnp.where(end <= place * PIECE, end, start)
    return start // PIECE


def key_chunk(slots_ref, first, pieces, *refs):
    last = slots_ref.shape[0] - 1
    slots = [slots_ref[jnp.clip(first + k, 0, last)] for k in range(pieces)]
    return slots, [jnp.concatenate([ref[s] for s in slots], axis=0) for ref in refs]


def stacked(ref, i, repeats):
    return jnp.concatenate(
        [ref[pl.ds(i * PIECE, PIECE), pl.ds(r * HD, HD)] for r in range(repeats)], axis=0)


def seen(lengths_ref, place, first, keys, cols):
    own = place * PIECE + lax.broadcasted_iota(jnp.int32, (1, cols), 1) % PIECE
    start = jnp.zeros((1, cols), jnp.int32)
    for end in ends_of(lengths_ref):
        start = jnp.where(end <= own, end, start)
    there = first * PIECE + lax.broadcasted_iota(jnp.int32, (keys, 1), 0)
    return (there <= own) & (there >= start)


CHUNK = 4


def forward_kernel(repeats, slots_ref, places_ref, lengths_ref, q_ref, k_ref, v_ref, low_ref, full_ref, lse_ref):
    cols = repeats * PIECE
    for i in range(q_ref.shape[0] // PIECE):
        place = places_ref[i]
        lo = key_span(place, lengths_ref)
        q = stacked(q_ref, i, repeats)

        def step(n, carry, lo=lo, place=place, q=q):
            top, total, acc = carry
            first = lo + n * CHUNK
            _, (k, v) = key_chunk(slots_ref, first, CHUNK, k_ref, v_ref)
            scores = dot_last(k, q) * HD**-0.5
            scores = jnp.where(seen(lengths_ref, place, first, CHUNK * PIECE, cols), scores, NEG)
            new = jnp.maximum(top, jnp.max(scores, axis=0, keepdims=True))
            weights = jnp.exp(scores - new)
            factor = jnp.exp(top - new)
            total = total * factor + jnp.sum(weights, axis=0, keepdims=True)
            return new, total, acc * factor + dot_first(v, weights.astype(BF16))

        top, total, acc = lax.fori_loop(
            0, (place - lo) // CHUNK + 1, step,
            (jnp.full((1, cols), NEG, F32), jnp.zeros((1, cols), F32), jnp.zeros((HD, cols), F32)))
        out = jnp.swapaxes(acc / total, 0, 1)
        lse_ref[0, pl.ds(i, 1), :] = top + jnp.log(total)
        for r in range(repeats):
            part = out[r * PIECE : (r + 1) * PIECE]
            full_ref[pl.ds(i * PIECE, PIECE), pl.ds(r * HD, HD)] = part
            low_ref[pl.ds(i * PIECE, PIECE), pl.ds(r * HD, HD)] = part.astype(BF16)


def attention_forward(query, kv, where):
    rows, pieces = query.shape[0], kv.shape[0]
    groups = kv.shape[2] // (2 * HD)
    wide = query.shape[1] // groups
    repeats = wide // HD
    spec = pl.BlockSpec((rows, wide), lambda g, *_: (0, g))
    return pl.pallas_call(
        functools.partial(forward_kernel, repeats),
        grid_spec=pltpu.PrefetchScalarGridSpec(
            num_scalar_prefetch=3,
            grid=(groups,),
            in_specs=[
                spec,
                pl.BlockSpec((pieces, PIECE, HD), lambda g, *_: (0, 0, g)),
                pl.BlockSpec((pieces, PIECE, HD), lambda g, *_: (0, 0, groups + g)),
            ],
            out_specs=[spec, spec, pl.BlockSpec((1, rows // PIECE, repeats * PIECE), lambda g, *_: (g, 0, 0))],
        ),
        out_shape=[
            jax.ShapeDtypeStruct(query.shape, BF16),
            jax.ShapeDtypeStruct(query.shape, F32),
            jax.ShapeDtypeStruct((groups, rows // PIECE, repeats * PIECE), F32),
        ],
        compiler_params=pltpu.CompilerParams(vmem_limit_bytes=48 << 20),
    )(*where, query, kv, kv)


def backward_kernel(
    repeats, slots_ref, places_ref, lengths_ref, q_ref, k_ref, v_ref, full_ref, grad_ref, lse_ref,
    dq_ref, dk_ref, dv_ref, key_acc, value_acc,
):
    cols = repeats * PIECE
    key_acc[...] = jnp.zeros_like(key_acc)
    value_acc[...] = jnp.zeros_like(value_acc)
    for i in range(q_ref.shape[0] // PIECE):
        place = places_ref[i]
        lo = key_span(place, lengths_ref)
        q, grad = stacked(q_ref, i, repeats), stacked(grad_ref, i, repeats)
        product = grad.astype(F32) * stacked(full_ref, i, repeats)
        delta = jnp.sum(jnp.swapaxes(product, 0, 1), axis=0, keepdims=True)
        lse = lse_ref[0, pl.ds(i, 1), :]

        def step(n, dq, lo=lo, place=place, q=q, grad=grad, delta=delta, lse=lse):
            first = lo + n * CHUNK
            slots, (k, v) = key_chunk(slots_ref, first, CHUNK, k_ref, v_ref)
            scores = dot_last(k, q) * HD**-0.5
            weights = jnp.where(
                seen(lengths_ref, place, first, CHUNK * PIECE, cols), jnp.exp(scores - lse), 0.0)
            back = (weights * (dot_last(v, grad) - delta)).astype(BF16)
            dk = dot(back, q)
            dv = dot(weights.astype(BF16), grad)
            for j, s in enumerate(slots):
                key_acc[s] += dk[j * PIECE : (j + 1) * PIECE]
                value_acc[s] += dv[j * PIECE : (j + 1) * PIECE]
            return dq + dot_first(k, back)

        dq = lax.fori_loop(0, (place - lo) // CHUNK + 1, step, jnp.zeros((HD, cols), F32))
        out = (jnp.swapaxes(dq, 0, 1) * HD**-0.5).astype(BF16)
        for r in range(repeats):
            dq_ref[pl.ds(i * PIECE, PIECE), pl.ds(r * HD, HD)] = out[r * PIECE : (r + 1) * PIECE]
    dk_ref[...] = (key_acc[...] * HD**-0.5).astype(BF16)
    dv_ref[...] = value_acc[...].astype(BF16)


def attention_backward(query, kv, full, lse, grad, where):
    rows, pieces = query.shape[0], kv.shape[0]
    groups = kv.shape[2] // (2 * HD)
    wide = query.shape[1] // groups
    repeats = wide // HD
    spec = pl.BlockSpec((rows, wide), lambda g, *_: (0, g))
    block = pl.BlockSpec((pieces, PIECE, HD), lambda g, *_: (0, 0, g))
    half = jax.ShapeDtypeStruct((pieces, PIECE, groups * HD), BF16)
    return pl.pallas_call(
        functools.partial(backward_kernel, repeats),
        grid_spec=pltpu.PrefetchScalarGridSpec(
            num_scalar_prefetch=3,
            grid=(groups,),
            in_specs=[
                spec, block, pl.BlockSpec((pieces, PIECE, HD), lambda g, *_: (0, 0, groups + g)), spec, spec,
                pl.BlockSpec((1, rows // PIECE, repeats * PIECE), lambda g, *_: (g, 0, 0)),
            ],
            out_specs=[spec, block, block],
            scratch_shapes=[pltpu.VMEM((pieces, PIECE, HD), F32)] * 2,
        ),
        out_shape=[jax.ShapeDtypeStruct(query.shape, BF16), half, half],
        compiler_params=pltpu.CompilerParams(vmem_limit_bytes=60 << 20),
    )(*where, query, kv, kv, full, grad, lse)


def tiles(total, size, body):
    if total == size:
        body(pl.ds(0, size))
    else:

        @pl.loop(0, total // size)
        def _(i):
            body(pl.ds(pl.multiple_of(i * size, size), size))


def shifted(c, by):
    if isinstance(c.start, int):
        return pl.ds(c.start + by, c.size)
    return pl.ds(pl.multiple_of(c.start + by, c.size), c.size)


def expert_kernel(
    chips, experts, ext_ref, up_own, up_other, down_own, down_other, cot_ref,
    shared_up, shared_down, cot_pair, cot_own, resid, gates, turned, low, full_out,
    output, hidden_grad, mixed_grad, out_part, up_part, down_part, din, dout, row_part, norm_pair, other_down,
    home_ref, routed_ref, din_ref, dout_ref, shared_act, shared_dab, hid, from_back, from_sum,
    in_ref, out_ref, ext, cot, rows_x, rows_dy, rows_act, rows_dab, both, result, back, deal, gate, take, take_gate,
    own_d, own_o, stage_d, stage_o, sib_d, sib_o, right_d, right_o, left_d, left_o,
    copy_sem, cot_sem, ag_r, ag_l, ag_sr, ag_sl, ss_r, ss_l, ss_sr, ss_sl,
    ex_sem, ss_ex, rs_r, rs_l, ss_rr, ss_rl, weight_sem, pair_sem, load_sem, y_send, y_recv,
):
    blk, core, at, sib = ring_info(chips)
    h = lax.axis_index("head")
    right, left = at(1), at(-1)
    half = chips // 2
    rows, wide = ext_ref.shape
    width = in_ref.shape[0]
    hidden = out_ref.shape[0]
    slots = rows_x.shape[0] // chips
    cut = rows // 2
    upper, lower = pl.ds(0, cut), pl.ds(cut, cut)

    barrier = pltpu.get_barrier_semaphore()
    for other in (right, left, sib):
        pl.semaphore_signal(barrier, inc=1, device_id={"blk": other}, device_id_type=MESH)
    pl.semaphore_signal(barrier, inc=1, device_id={"head": 1 - h}, device_id_type=MESH)
    pl.semaphore_wait(barrier, 4)

    def remote(src, dst, ssem, rsem, dev):
        return pltpu.make_async_remote_copy(
            src_ref=src, dst_ref=dst, send_sem=ssem, recv_sem=rsem,
            device_id={"blk": dev}, device_id_type=MESH)

    def hop_right(part, k, s):
        ref = ext.at[at(1 - s), part]
        return remote(ref, ref, ss_r.at[k, s], ag_r.at[k, s], right)

    def hop_left(part, k, s):
        ref = ext.at[at(s - 1), part]
        return remote(ref, ref, ss_l.at[k, s], ag_l.at[k, s], left)

    def over_right(part, k, s):
        ref = ext.at[at(-s), part]
        return remote(ref, ref, ss_sr.at[k, s], ag_sr.at[k, s], sib)

    def over_left(part, k, s):
        ref = ext.at[at(s), part]
        return remote(ref, ref, ss_sl.at[k, s], ag_sl.at[k, s], sib)

    def place_of(g, j):
        return at(-g) if j == 0 else at(g)

    def cot_copy(g, j):
        there = place_of(g, j)
        slot = lax.rem(g, 2)
        return pltpu.make_async_copy(
            cot_ref.at[pl.ds(there - core, 2)], cot.at[slot, j], cot_sem.at[slot, j])

    def exchange_d(g, j):
        return remote(stage_d.at[j], sib_d.at[lax.div(place_of(g, j), 2)], ss_ex.at[0, j, g], ex_sem.at[0, j, g], sib)

    def exchange_o(g, j):
        return remote(stage_o.at[j], sib_o.at[lax.div(place_of(g, j), 2)], ss_ex.at[1, j, g], ex_sem.at[1, j, g], sib)

    mine = pltpu.make_async_copy(ext_ref, ext.at[blk], copy_sem)
    mine.start()
    cot_copy(0, 0).start()
    weights = []
    for i, (up, down) in ((h, (up_own, down_own)), (1 - h, (up_other, down_other))):
        size = up.shape[0]
        start = pl.multiple_of(i * size, size)
        weights.append((up, in_ref.at[pl.ds(start, size)]))
        weights.append((down, out_ref.at[:, pl.ds(start, size)]))
    weights = [pltpu.make_async_copy(a, b, weight_sem.at[i]) for i, (a, b) in enumerate(weights)]
    for copy in weights:
        copy.start()
    mine.wait()
    for k, part in ((0, upper), (1, lower)):
        hop_right(part, k, 1).start()
        hop_left(part, k, 1).start()
        over_right(part, k, 0).start()
    own_norm = ext.at[blk, :, pl.ds(0, width)]
    keep = pltpu.make_async_copy(own_norm, norm_pair.at[h], pair_sem.at[0])
    keep.start()
    swapped = pltpu.make_async_remote_copy(
        src_ref=own_norm, dst_ref=norm_pair.at[h], send_sem=pair_sem.at[1], recv_sem=pair_sem.at[2],
        device_id={"head": 1 - h}, device_id_type=MESH)
    swapped.start()
    for copy in weights:
        copy.wait()

    lane = lax.broadcasted_iota(jnp.int32, (2 * rows, 128), 1)
    token_row = lax.broadcasted_iota(jnp.int32, (2 * rows, 2 * rows), 0)
    token_col = lax.broadcasted_iota(jnp.int32, (2 * rows, 2 * rows), 1)
    same = (token_row < rows) == (token_col < rows)
    triangle = jnp.where((token_row > token_col) & same, 1.0, 0.0).astype(BF16)
    offset = jnp.float32(slots // 2)
    shift_col = jnp.where(lax.broadcasted_iota(jnp.int32, (2 * rows, 1), 0) < rows, 0.0, offset)
    shift_row = jnp.where(lax.broadcasted_iota(jnp.int32, (1, 2 * rows), 1) < rows, 0.0, offset)
    slot_id = lax.broadcasted_iota(jnp.int32, (slots, 2 * rows), 0).astype(F32)
    lane_row = lax.broadcasted_iota(jnp.int32, (128, 128), 0)
    pick_mask = jnp.where(lane_row == experts + blk, 1.0, 0.0).astype(BF16)
    pick_gate = jnp.where(lane_row == blk, 1.0, 0.0).astype(BF16)
    lane_col = lax.broadcasted_iota(jnp.int32, (8, 128), 1)
    mask_row = jnp.where(lane_col == experts + blk, 1.0, 0.0).astype(BF16)
    gate_row = jnp.where(lane_col == blk, 1.0, 0.0).astype(BF16)

    def arrive(s):
        last = isinstance(s, int) and s == half
        hop_right(upper, 0, s).wait_recv()
        if not last:
            hop_right(upper, 0, s + 1).start()
        over_right(upper, 0, s).start()
        hop_left(lower, 1, s).wait_recv()
        if not last:
            hop_left(lower, 1, s + 1).start()
        over_left(lower, 1, s).start()
        if last:
            return
        hop_right(lower, 1, s).wait_recv()

        @pl.when(s < half - 1)
        def _():
            hop_right(lower, 1, s + 1).start()

        over_right(lower, 1, s).start()
        hop_left(upper, 0, s).wait_recv()

        @pl.when(s < half - 1)
        def _():
            hop_left(upper, 0, s + 1).start()

        over_left(upper, 0, s).start()

    def work(g, count, base, first):
        turn = lax.rem(g, 2)
        size = count * slots
        group = pl.ds(base, size)
        part = pl.ds(0, size)
        firsts = [place_of(g, j) - core for j in range(count)]
        for j in range(count):
            lanes = ext[pl.ds(firsts[j], 2), :, pl.ds(width, 128)].reshape(2 * rows, 128)
            chosen = dot(lanes, pick_mask)
            rank = dot(triangle, chosen.astype(BF16))
            spread = jnp.where((rank + shift_col == lane.astype(F32)) & (chosen > 0.5), 1.0, 0.0).astype(BF16)
            deal[j] = spread.reshape(2, rows, 128)
            gate[j] = dot(lanes, pick_gate).reshape(2, rows, 128)
            chosen_row = dot_last(mask_row, lanes)
            rank_row = dot_last(chosen_row.astype(BF16), triangle)
            weight_row = dot_last(gate_row, lanes)
            taken = jnp.where((rank_row[:1] + shift_row == slot_id) & (chosen_row[:1] > 0.5), 1.0, 0.0)
            take[j] = taken.astype(BF16)
            take_gate[j] = (taken * weight_row[:1]).astype(BF16)
        for j in range(count):
            cot_copy(g, j).wait()
            where = pl.ds(pl.multiple_of(base + j * slots, slots), slots)

            def pick_rows(c, j=j, where=where):
                rows_x[where, c] = dot(
                    take[j], ext[pl.ds(firsts[j], 2), :, c].reshape(2 * rows, c.size)).astype(BF16)
                rows_dy[where, c] = dot(take_gate[j], cot[turn, j, :, :, c].reshape(2 * rows, c.size)).astype(BF16)

            for t in range(2):
                pick_rows(pl.ds(t * (width // 2), width // 2))

        def hidden_tile(c):
            high = shifted(c, hidden)
            x = rows_x[group]
            gate_part = dot(x, in_ref[:, c])
            lift = dot(x, in_ref[:, high])
            both[part, c] = gate_part
            both[part, high] = lift
            rows_act[group, c] = (jax.nn.silu(gate_part) * lift).astype(BF16)

        for t in range(2):
            hidden_tile(pl.ds(t * (hidden // 2), hidden // 2))

        def result_tile(c):
            result[part, c] = dot(rows_act[group], out_ref[:, c]).astype(BF16)

        for t in range(2):
            result_tile(pl.ds(t * (width // 2), width // 2))

        def grad_tile(c):
            high = shifted(c, hidden)
            da = dot_last(rows_dy[group], out_ref[c, :])
            gate_part, lift = both[part, c], both[part, high]
            sig = jax.nn.sigmoid(gate_part)
            rows_dab[group, c] = (da * lift * sig * (1.0 + gate_part * (1.0 - sig))).astype(BF16)
            rows_dab[group, high] = (da * gate_part * sig).astype(BF16)

        for t in range(2):
            grad_tile(pl.ds(t * (hidden // 2), hidden // 2))

        def back_tile(c):
            back[part, c] = dot_last(rows_dab[group], in_ref[c, :]).astype(BF16)

        for t in range(2):
            back_tile(pl.ds(t * (width // 2), width // 2))
        if first is not None:

            @pl.when(first)
            def _():
                for j in range(2):
                    exchange_d(g - 1, j).wait_send()
                    exchange_o(g - 1, j).wait_send()

            @pl.when(jnp.logical_not(first))
            def _():
                exchange_d(g - 1, 0).wait_send()
                exchange_o(g - 1, 0).wait_send()

        for j in range(count):
            chip = lax.div(firsts[j], 2)
            for which, to_d, to_o in (
                (core, own_d.at[chip], own_o.at[chip]),
                (1 - core, stage_d.at[j], stage_o.at[j]),
            ):
                from_slots = pl.ds(j * slots, slots)
                dealer = deal[j, which]
                share = gate[j, which]
                total = jnp.zeros((rows, 1), F32)
                for t in range(width // 512):
                    c = pl.ds(t * 512, 512)
                    home_rows = dot(dealer, result[from_slots, c])
                    to_o[:, c] = (home_rows * share[:, :1]).astype(BF16)
                    total = total + jnp.sum(
                        home_rows * cot[turn, j, which, :, c].astype(F32), axis=1, keepdims=True)
                    to_d[:, c] = dot(dealer, back[from_slots, c]).astype(BF16)
                high = total.astype(BF16).astype(F32)
                own_lane = lane[:rows]
                lanes = jnp.where(own_lane == blk, high, jnp.where(own_lane == experts + blk, total - high, 0.0))
                to_d[:, pl.ds(width, 128)] = lanes.astype(BF16)
            exchange_d(g, j).start()
            exchange_o(g, j).start()

    over_right(upper, 0, 0).wait_recv()
    over_right(lower, 1, 0).wait_recv()
    cot_copy(1, 0).start()
    cot_copy(1, 1).start()
    work(0, 1, 0, None)

    @pl.loop(1, half)
    def _(g):
        arrive(g)
        over_right(upper, 0, g).wait_recv()
        over_right(lower, 1, g).wait_recv()
        over_left(lower, 1, g).wait_recv()
        over_left(upper, 0, g).wait_recv()
        cot_copy(g + 1, 0).start()

        @pl.when(g < half - 1)
        def _():
            cot_copy(g + 1, 1).start()

        work(g, 2, pl.multiple_of(slots + (g - 1) * 2 * slots, slots), g > 1)

    arrive(half)
    over_right(upper, 0, half).wait_recv()
    over_left(lower, 1, half).wait_recv()
    work(half, 1, (2 * half - 1) * slots, True)

    arrays = ((0, own_d, sib_d, right_d, left_d, home_ref), (1, own_o, sib_o, right_o, left_o, routed_ref))
    arrived = set()

    def join(a, own, other, d, part, into, received):
        g, j = (d, 1) if 0 < d < half else (abs(d), 0)
        if (a, g, j) not in arrived:
            arrived.add((a, g, j))
            (exchange_d, exchange_o)[a](g, j).wait_recv()
        chip = lax.div(at(d), 2)

        def add(c):
            total = own[chip, c].astype(F32) + other[chip, c].astype(F32)
            for ref in received:
                total = total + ref[c].astype(F32)
            into[c] = total.astype(into.dtype)

        @pl.loop(0, cut // 16)
        def _(i):
            add(pl.ds(pl.multiple_of(part.start + i * 16, 16), 16))

    def pass_right(a, src, buf, k, part, s):
        return remote(src.at[part], buf.at[s - 1, part], ss_rr.at[a, k, s], rs_r.at[a, k, s], right)

    def pass_left(a, src, buf, k, part, s):
        return remote(src.at[part], buf.at[s - 1, part], ss_rl.at[a, k, s], rs_l.at[a, k, s], left)

    ways = (
        (0, upper, 1, half), (1, lower, -1, half), (1, lower, 1, half - 1), (0, upper, -1, half - 1),
    )
    sent = []

    def scatter_step(a, s):
        _, own, other, to_right, to_left, _ = arrays[a]
        for k, part, way, hops in ways:
            if s > hops:
                continue
            make, buf = (pass_right, to_right) if way > 0 else (pass_left, to_left)
            d = way * (hops - s + 1)
            if d == -half:
                d = half
            if s == 1:
                src = own.at[lax.div(at(d), 2)]
                join(a, own, other, d, part, src, ())
            else:
                src = buf.at[s - 2]
                make(a, src, buf, k, part, s - 1).wait_recv()
                join(a, own, other, d, part, src, (src,))
            copy = make(a, src, buf, k, part, s)
            copy.start()
            sent.append(copy)

    def scatter_finish(a):
        _, own, other, to_right, to_left, into = arrays[a]
        for k, part in ((0, upper), (1, lower)):
            last_right, last_left = half - k, half - 1 + k
            pass_right(a, own.at[0], to_right, k, part, last_right).wait_recv()
            pass_left(a, own.at[0], to_left, k, part, last_left).wait_recv()
            join(a, own, other, 0, part, into, (to_right.at[last_right - 1], to_left.at[last_left - 1]))

    loads = 0

    def move(src, dst):
        nonlocal loads
        copy = pltpu.make_async_copy(src, dst, load_sem.at[loads])
        loads += 1
        copy.start()
        return copy

    def cross(i, src, dst):
        return pltpu.make_async_remote_copy(
            src_ref=src, dst_ref=dst, send_sem=y_send.at[i], recv_sem=y_recv.at[i],
            device_id={"head": 1 - h}, device_id_type=MESH)

    theirs = pl.ds(pl.multiple_of((1 - h) * rows, rows), rows)
    ours = pl.ds(pl.multiple_of(h * rows, rows), rows)
    keep.wait()
    swapped.wait()
    shared_loads = [
        move(shared_up, in_ref), move(shared_down, out_ref), move(cot_pair, back),
        move(norm_pair.at[0], result.at[pl.ds(0, rows)]), move(norm_pair.at[1], result.at[pl.ds(rows, rows)])]
    scatter_step(0, 1)

    def weight_in(c):
        din_ref[c, :] = dot_first(rows_x[:, c], rows_dab[...]).astype(BF16)

    tiles(width, 256, weight_in)
    din_out = move(din_ref, din)
    load_out = move(full_out, rows_x.at[pl.ds(0, low.shape[1])])
    scatter_step(0, 2)

    for copy in shared_loads:
        copy.wait()

    def shared_tile(c):
        high = shifted(c, hidden)
        gate_part = dot(result[...], in_ref[:, c])
        lift = dot(result[...], in_ref[:, high])
        sig = jax.nn.sigmoid(gate_part)
        shared_act[:, c] = (gate_part * sig * lift).astype(BF16)
        da = dot_last(back[...], out_ref[c, :])
        shared_dab[:, c] = (da * lift * sig * (1.0 + gate_part * (1.0 - sig))).astype(BF16)
        shared_dab[:, high] = (da * gate_part * sig).astype(BF16)

    tiles(hidden, 256, shared_tile)
    to_back, to_sum = cot.at[0, 0, 0], cot.at[0, 0, 1]

    def back_part(c):
        to_back[:, c] = dot_last(shared_dab[theirs, :], in_ref[c, :]).astype(BF16)

    tiles(width, 512, back_part)
    swap_back = cross(0, to_back, from_back)
    swap_back.start()

    def weight_out(c):
        dout_ref[c, :] = dot_first(rows_act[:, c], rows_dy[...]).astype(BF16)

    tiles(hidden, 256, weight_out)
    dout_out = move(dout_ref, dout)
    scatter_step(0, 3)
    scatter_step(1, 1)

    def sum_part(c):
        to_sum[:, c] = dot(shared_act[theirs, :], out_ref[:, c]).astype(BF16)

    tiles(width, 512, sum_part)
    swap_sum = cross(1, to_sum, from_sum)
    swap_sum.start()
    din_out.wait()
    dout_out.wait()
    swap_down = cross(3, dout.at[:, pl.ds(pl.multiple_of((1 - h) * (width // 2), 128), width // 2)], other_down)
    swap_down.start()

    def shared_in(c):
        din_ref[c, :] = dot_first(result[:, c], shared_dab[...]).astype(BF16)

    tiles(width, 256, shared_in)
    up_out = move(din_ref, up_part)
    scatter_step(0, 4)
    scatter_step(1, 2)

    def shared_out(c):
        dout_ref[c, :] = dot_first(shared_act[:, c], back[...]).astype(BF16)

    tiles(hidden, 256, shared_out)
    down_out = move(dout_ref, down_part)
    swap_back.wait_recv()
    scatter_finish(0)

    lanes = home_ref[:, pl.ds(width, 128)].astype(BF16)
    row_id = lax.broadcasted_iota(jnp.int32, (128, 128), 0)
    col_id = lax.broadcasted_iota(jnp.int32, (128, 128), 1)
    fold = jnp.where((row_id == col_id) | (row_id == col_id + experts), 1.0, 0.0).astype(BF16)
    weighted = gates[...] * dot(lanes, fold)
    logit_grad = (weighted - gates[...] * jnp.sum(weighted, axis=1, keepdims=True)).astype(BF16)
    short = logit_grad[:, : turned.shape[0]]

    def norm_part(c):
        hidden_grad[:, c] = (
            home_ref[:, c] + from_back[:, c].astype(F32) + dot_last(shared_dab[ours, :], in_ref[c, :])
            + dot(short, turned[:, c].astype(BF16)))
        row_part[:, c] = dot_first(logit_grad, ext[blk, :, c])

    tiles(width, 512, norm_part)

    def norm_rows(n, total):
        part = pl.ds(pl.multiple_of(n * 32, 32), 32)
        x, up = resid[part, :], hidden_grad[part, :]
        scaler = lax.rsqrt(jnp.mean(x * x, axis=1, keepdims=True) + EPS)
        normed = x * scaler
        scaled = up * turned[pl.ds(experts + 1, 1), :]
        grad = cot_own[part, :].astype(F32) + scaler * (
            scaled - normed * jnp.mean(scaled * normed, axis=1, keepdims=True))
        hidden_grad[part, :] = grad
        hid[h, part, :] = grad.astype(BF16)
        return total + jnp.sum(up * normed, axis=0, keepdims=True)

    gain = lax.fori_loop(0, rows // 32, norm_rows, jnp.zeros((1, width), F32))
    swap_hid = cross(2, hid.at[h], hid.at[h])
    swap_hid.start()
    scatter_step(1, 3)
    row_part[pl.ds(experts + 1, 1), :] = gain
    load_out.wait()
    inner = low.shape[1]
    full = rows_x.at[pl.ds(0, inner)]

    def mixed_tile(who, where):
        for t in range(inner // 256):
            c = pl.ds(t * 256, 256)
            mixed_grad[where, c] = dot_last(hid[who], full[c, :]).astype(BF16)

    mixed_tile(h, ours)
    scatter_step(1, 4)
    swap_hid.wait_recv()
    mixed_tile(1 - h, theirs)

    def out_tile(c):
        rows_dy[c, :] = (
            dot_first(low[pl.ds(0, rows), c], hid[0]) + dot_first(low[pl.ds(rows, rows), c], hid[1])).astype(BF16)

    for t in range(inner // 256):
        out_tile(pl.ds(t * 256, 256))
    part_out = move(rows_dy.at[pl.ds(0, inner)], out_part)
    swap_sum.wait_recv()
    scatter_finish(1)

    def output_tile(c):
        output[:, c] = (
            resid[:, c] + routed_ref[:, c] + from_sum[:, c].astype(F32)
            + dot(shared_act[ours, :], out_ref[:, c])).astype(BF16)

    tiles(width, 512, output_tile)
    for copy in (swap_back, swap_sum, swap_hid, swap_down):
        copy.wait_send()
    swap_down.wait_recv()
    for copy in (up_out, down_out, part_out):
        copy.wait()
    for copy in sent:
        copy.wait_send()
    exchange_d(half, 0).wait_send()
    exchange_o(half, 0).wait_send()
    for k, part in ((0, upper), (1, lower)):
        over_right(part, k, 0).wait_send()
        for s in range(1, half + 1):
            if s <= half - k:
                hop_right(part, k, s).wait_send()
                over_right(part, k, s).wait_send()
            if s <= half - 1 + k:
                hop_left(part, k, s).wait_send()
                over_left(part, k, s).wait_send()


def experts_fused(
    ext, weights, cot_all, shared, cot_pair, cot_own, resid, gates, turned, low, full_out, blks, capacity, collective_id,
):
    chips, half = blks // 2, blks // 4
    rows, wide = ext.shape
    width, hidden = 2 * weights[0].shape[0], weights[2].shape[0]
    count = blks * capacity
    group = 4 * capacity
    inner = low.shape[1]
    dma = pltpu.SemaphoreType.DMA
    vmem = pl.BlockSpec(memory_space=pltpu.VMEM)
    anywhere = pl.BlockSpec(memory_space=pl.ANY)

    def bf16(*shape):
        return pltpu.VMEM(shape, BF16)

    def f32(*shape):
        return pltpu.VMEM(shape, F32)

    out = [
        ((rows, width), BF16, vmem), ((rows, width), F32, vmem), ((2 * rows, inner), BF16, vmem),
        ((inner, width), BF16, anywhere), ((width, 2 * hidden), BF16, anywhere), ((hidden, width), BF16, anywhere),
        ((width, 2 * hidden), BF16, anywhere), ((hidden, width), BF16, anywhere), ((128, width), F32, vmem),
        ((2, rows, width), BF16, anywhere), ((hidden, width // 2), BF16, anywhere),
    ]
    return pl.pallas_call(
        functools.partial(expert_kernel, chips, blks),
        out_shape=[jax.ShapeDtypeStruct(s, t) for s, t, _ in out],
        in_specs=[anywhere] * 9 + [vmem] * 5 + [anywhere],
        out_specs=[space for _, _, space in out],
        scratch_shapes=[
            f32(rows, wide), f32(rows, width), bf16(width, 2 * hidden), bf16(hidden, width),
            bf16(2 * rows, hidden), bf16(2 * rows, 2 * hidden), bf16(2, rows, width), bf16(rows, width), bf16(rows, width),
            bf16(width, 2 * hidden), bf16(hidden, width),
            bf16(blks, rows, wide), bf16(2, 2, 2, rows, width),
            bf16(count, width), bf16(count, width), bf16(count, hidden), bf16(count, 2 * hidden),
            f32(group, 2 * hidden), bf16(group, width), bf16(group, width),
            bf16(2, 2, rows, 128), f32(2, 2, rows, 128), bf16(2, 128, 2 * rows), bf16(2, 128, 2 * rows),
            bf16(chips, rows, wide), bf16(chips, rows, width), bf16(2, rows, wide), bf16(2, rows, width),
            bf16(chips, rows, wide), bf16(chips, rows, width),
            bf16(half, rows, wide), bf16(half, rows, width), bf16(half, rows, wide), bf16(half, rows, width),
            dma(()), dma((2, 2)),
        ] + [dma((2, half + 1))] * 8 + [dma((2, 2, half + 1))] * 2 + [dma((2, 2, half + 1))] * 4
        + [dma((4,)), dma((3,)), dma((11,)), dma((4,)), dma((4,))],
        compiler_params=pltpu.CompilerParams(
            collective_id=collective_id, has_side_effects=True, vmem_limit_bytes=63 << 20),
    )(ext, *weights, cot_all, *shared, cot_pair, cot_own, resid, gates, turned, low, full_out)


class Ring:
    def __init__(self, info, chips, chunks, first, sems):
        self.blk, self.at, self.sib = info
        self.half = chips // 2
        self.chunks, self.first = chunks, first
        self.send_r, self.recv_r, self.send_l, self.recv_l, self.send_s, self.recv_s = sems

    def hops(self, c):
        return self.half - c % 2, self.half - 1 + c % 2

    def copy(self, ref, ssem, rsem, dev):
        return pltpu.make_async_remote_copy(
            src_ref=ref, dst_ref=ref, send_sem=ssem, recv_sem=rsem,
            device_id={"blk": dev}, device_id_type=MESH)

    def right(self, c, s):
        i = self.first + c
        return self.copy(self.chunks[c](self.at(1 - s)), self.send_r.at[i, s], self.recv_r.at[i, s], self.at(1))

    def left(self, c, s):
        i = self.first + c
        return self.copy(self.chunks[c](self.at(s - 1)), self.send_l.at[i, s], self.recv_l.at[i, s], self.at(-1))

    def over(self, c, d):
        i, k = self.first + c, d + self.half
        return self.copy(self.chunks[c](self.at(d)), self.send_s.at[i, k], self.recv_s.at[i, k], self.sib)

    def start(self, c):
        self.right(c, 1).start()
        self.left(c, 1).start()
        self.over(c, 0).start()

    def step(self, s):
        for c in range(len(self.chunks)):
            rh, lh = self.hops(c)
            if s <= rh:
                self.right(c, s).wait_recv()
                if s < rh:
                    self.right(c, s + 1).start()
                self.over(c, -s).start()
            if s <= lh:
                self.left(c, s).wait_recv()
                if s < lh:
                    self.left(c, s + 1).start()
                self.over(c, s).start()

    def end(self):
        for c in range(len(self.chunks)):
            rh, lh = self.hops(c)
            for d in range(-rh, lh + 1):
                self.over(c, d).wait_recv()

    def flush(self):
        for c in range(len(self.chunks)):
            rh, lh = self.hops(c)
            for s in range(1, rh + 1):
                self.right(c, s).wait_send()
            for s in range(1, lh + 1):
                self.left(c, s).wait_send()
            for d in range(-rh, lh + 1):
                self.over(c, d).wait_send()


def front_kernel(
    chips, experts,
    order_ref, lengths_ref, routes, router, gain_one, gain_two, tokens, cotangent, w_query, w_key, w_value, w_out,
    shared_up, shared_down, expert_up, expert_down,
    n1_out, query_out, kv_out, first_out, out_out, up_w, down_w, cot, cot_pair, expert_in, expert_out,
    low_out, full_out, lse, resid, ext, gates, short, slots_ref,
    small, n1, query, kv, first_w, out_w, low, full, turned, pair, to_other, from_other,
    send_r, recv_r, send_l, recv_l, send_s, recv_s, own_sem, y_send, y_recv, store_sem,
):
    h = lax.axis_index("head")
    blk, core, at, sib = ring_info(chips)
    half = chips // 2
    rows, width = tokens.shape
    qw, kw = w_query.shape[1] // 2, w_key.shape[1] // 2
    sw = shared_up.shape[1] // 4
    barrier = pltpu.get_barrier_semaphore()
    for other in (at(1), at(-1), sib):
        pl.semaphore_signal(barrier, inc=1, device_id={"blk": other}, device_id_type=MESH)
    pl.semaphore_signal(barrier, inc=1, device_id={"head": 1 - h}, device_id_type=MESH)
    pl.semaphore_wait(barrier, 4)

    wide = lax.broadcasted_iota(jnp.int32, (experts, 128), 1)
    column = lax.broadcasted_iota(jnp.int32, (experts, 128), 0)
    block = dot_first(router[...], jnp.where(wide == column, 1.0, 0.0).astype(BF16))
    for n, gain in ((0, gain_one), (1, gain_two)):
        spot = jnp.where(lax.broadcasted_iota(jnp.int32, (1, 128), 1) == experts + n, 1.0, 0.0).astype(BF16)
        block = block + dot_first(gain[...], spot)
    small[...] = block.astype(BF16)

    def lanes_of(start, size):
        return pl.ds(pl.multiple_of(start, 128), size)

    def halves(i, j):
        return [
            (w_query.at[:, lanes_of(i * qw, qw)], first_w.at[j, blk, :, pl.ds(0, qw)]),
            (w_key.at[:, lanes_of(i * kw, kw)], first_w.at[j, blk, :, pl.ds(qw, kw)]),
            (w_value.at[:, lanes_of(i * kw, kw)], first_w.at[j, blk, :, pl.ds(qw + kw, kw)]),
            (small, first_w.at[j, blk, :, pl.ds(qw + 2 * kw, small.shape[1])]),
            (tokens, pair.at[j]),
            (shared_up.at[:, lanes_of(i * sw, sw)], up_w.at[j, blk, :, pl.ds(0, sw)]),
            (shared_up.at[:, lanes_of((2 + i) * sw, sw)], up_w.at[j, blk, :, pl.ds(sw, sw)]),
            (cotangent, cot_pair.at[j]),
        ]

    whole = [(expert_up, expert_in), (expert_down, expert_out)]

    stores = []

    def store(src, dst):
        copy = pltpu.make_async_copy(src, dst, store_sem.at[len(stores)])
        copy.start()
        stores.append(copy)

    own = [pltpu.make_async_copy(a, b, own_sem.at[i]) for i, (a, b) in enumerate(halves(h, h))]
    own.append(pltpu.make_async_copy(w_out, out_w.at[blk], own_sem.at[len(own)]))
    own.append(pltpu.make_async_copy(shared_down, down_w.at[blk], own_sem.at[len(own)]))
    own.append(pltpu.make_async_copy(cotangent, cot.at[blk], own_sem.at[len(own)]))
    swaps = [
        pltpu.make_async_remote_copy(
            src_ref=a, dst_ref=b, send_sem=y_send.at[i], recv_sem=y_recv.at[i],
            device_id={"head": 1 - h}, device_id_type=MESH)
        for i, (a, b) in enumerate(halves(1 - h, h) + whole)
    ]
    for i in range(5):
        swaps[i].start()
    for i in (0, 1, 2, 3, 8, 4):
        own[i].start()

    info = (blk, at, sib)
    sems = (send_r, recv_r, send_l, recv_l, send_s, recv_s)

    def row_cuts(ref, *sizes):
        start, chunks = 0, []
        for size in sizes:
            chunks.append(lambda b, start=start, size=size: ref.at[b, pl.ds(start, size)])
            start += size
        return chunks

    ring_w = Ring(info, chips, [lambda b: first_w.at[h, b], lambda b: first_w.at[1 - h, b]], 0, sems)
    out_rows, down_rows = w_out.shape[0], shared_down.shape[0]
    ring_o = Ring(info, chips, row_cuts(out_w, 32, out_rows - 32), 2, sems)
    ring_kv = Ring(info, chips, [lambda b: kv.at[2 * b], lambda b: kv.at[2 * b + 1]], 4, sems)
    ring_u = Ring(info, chips, [lambda b: up_w.at[h, b], lambda b: up_w.at[1 - h, b]], 6, sems)
    ring_d = Ring(info, chips, row_cuts(down_w, down_rows // 2, down_rows // 2), 8, sems)
    ring_c = Ring(info, chips, row_cuts(cot, rows // 2, rows // 2), 10, sems)

    for i in (0, 1, 2, 3):
        own[i].wait()
    ring_w.start(0)
    own[10].start()
    own[10].wait()
    ring_c.start(0)
    ring_c.start(1)
    own[8].wait()
    for i in range(4):
        swaps[i].wait_recv()
    ring_w.start(1)
    ring_o.start(0)
    ring_o.start(1)
    for i in (5, 6, 9, 7):
        own[i].start()
    for i in range(5, 10):
        swaps[i].start()
    for s in range(1, half + 1):
        ring_w.step(s)
        ring_o.step(s)
    ring_c.step(1)
    ring_w.end()
    store(first_w, first_out)
    own[4].wait()
    swaps[4].wait_recv()

    @pl.loop(0, slots_ref.shape[0])
    def _(j):
        slot = jnp.int32(0)
        for n in range(order_ref.shape[0]):
            there = 2 * (n % (2 * chips)) + n // (2 * chips)
            slot = jnp.maximum(slot, jnp.where(order_ref[n] == j, there, 0))
        slots_ref[j] = slot

    small_cols = first_w[:, :, :, pl.ds(qw + 2 * kw, 128)].reshape(width, 128)
    turned[...] = jnp.swapaxes(small_cols.astype(F32), 0, 1)
    short[...] = turned[pl.ds(0, short.shape[0]), :]

    @pl.loop(0, 2 * rows // 64)
    def _(i):
        x = pair[lax.div(i, rows // 64), pl.ds(pl.multiple_of(lax.rem(i, rows // 64) * 64, 64), 64), :].astype(F32)
        scaled = x * lax.rsqrt(jnp.mean(x * x, axis=1, keepdims=True) + EPS) * turned[pl.ds(experts, 1), :]
        n1[pl.ds(pl.multiple_of(i * 64, 64), 64), :] = scaled.astype(BF16)

    def project(start, size):
        weights = first_w[:, :, :, pl.ds(start, size)].reshape(width, size)
        return dot(n1[...], weights).astype(BF16)

    for t in range(2 * kw // 256):
        part = project(qw + t * 256, 256)
        for i in range(2):
            kv[2 * blk + i, :, pl.ds(t * 256, 256)] = part[i * rows : (i + 1) * rows]
    ring_kv.start(0)
    ring_kv.start(1)
    for t in range(qw // 256):
        query[:, pl.ds(t * 256, 256)] = project(t * 256, 256)
    for i in (5, 6, 9):
        own[i].wait()
    swaps[5].wait_recv()
    swaps[6].wait_recv()
    for s in range(1, half + 1):
        ring_kv.step(s)
        if s == half - 1:
            ring_c.step(2)
            for ring in (ring_u, ring_d):
                ring.start(0)
                ring.start(1)
    ring_kv.end()
    store(kv, kv_out)
    store(n1, n1_out)
    store(query, query_out)

    groups, repeats = kw // HD, qw // kw
    cols = repeats * PIECE
    pieces = slots_ref.shape[0]
    need = pieces // 2 + 1
    chunk = 6
    chunks = -(-need // chunk)
    later = [(ring_u, 1), (ring_d, 1), (ring_c, 3), (ring_u, 2), (ring_d, 2), (ring_c, 4)]
    turns = 0
    for i in range(2):
        place = order_ref[i * 2 * chips + blk]
        for g in range(groups):
            q = jnp.concatenate(
                [query[pl.ds(i * PIECE, PIECE), pl.ds((g * repeats + r) * HD, HD)] for r in range(repeats)], axis=0)

            def step(n, carry, place=place, g=g, q=q):
                top, total, acc = carry
                first = place + 1 - chunks * chunk + n * chunk
                _, (k, v) = key_chunk(
                    slots_ref, first, chunk, kv.at[:, :, pl.ds(g * HD, HD)], kv.at[:, :, pl.ds((groups + g) * HD, HD)])
                scores = dot_last(k, q) * HD**-0.5
                scores = jnp.where(seen(lengths_ref, place, first, chunk * PIECE, cols), scores, NEG)
                new = jnp.maximum(top, jnp.max(scores, axis=0, keepdims=True))
                weights = jnp.exp(scores - new)
                factor = jnp.exp(top - new)
                total = total * factor + jnp.sum(weights, axis=0, keepdims=True)
                return new, total, acc * factor + dot_first(v, weights.astype(BF16))

            top, total, acc = lax.fori_loop(
                0, chunks, step,
                (jnp.full((1, cols), NEG, F32), jnp.zeros((1, cols), F32), jnp.zeros((HD, cols), F32)))
            out = jnp.swapaxes(acc / total, 0, 1)
            lse[g, pl.ds(i, 1), :] = top + jnp.log(total)
            for r in range(repeats):
                part = out[r * PIECE : (r + 1) * PIECE]
                full[pl.ds(i * PIECE, PIECE), pl.ds((g * repeats + r) * HD, HD)] = part
                low[pl.ds(i * PIECE, PIECE), pl.ds((g * repeats + r) * HD, HD)] = part.astype(BF16)
            turns += 1
            if turns % 2 == 0:
                for ring, s in later[:3]:
                    ring.step(s)
                later = later[3:]

    ring_o.end()
    store(out_w, out_out)
    store(low, low_out)
    store(full, full_out)
    theirs = pl.ds(pl.multiple_of((1 - h) * rows, rows), rows)
    ours = pl.ds(pl.multiple_of(h * rows, rows), rows)

    def mixed(where, c):
        return dot(low[where, :], out_w[:, :, c].reshape(qw, c.size))

    for t in range(width // 512):
        c = pl.ds(t * 512, 512)
        to_other[:, c] = mixed(theirs, c).astype(BF16)
    swap_mixed = pltpu.make_async_remote_copy(
        src_ref=to_other, dst_ref=from_other, send_sem=y_send.at[10], recv_sem=y_recv.at[10],
        device_id={"head": 1 - h}, device_id_type=MESH)
    swap_mixed.start()
    for t in range(width // 512):
        c = pl.ds(t * 512, 512)
        resid[:, c] = pair[h, :, c].astype(F32) + mixed(ours, c)
    for ring in (ring_u, ring_d):
        ring.step(3)
    swap_mixed.wait_recv()

    @pl.loop(0, rows // 32)
    def _(i):
        part = pl.ds(pl.multiple_of(i * 32, 32), 32)
        x = resid[part, :] + from_other[part, :].astype(F32)
        resid[part, :] = x
        scaled = x * lax.rsqrt(jnp.mean(x * x, axis=1, keepdims=True) + EPS) * turned[pl.ds(experts + 1, 1), :]
        ext[part, pl.ds(0, width)] = scaled.astype(BF16)

    logits = dot_last(ext[:, pl.ds(0, width)], turned[...].astype(BF16))
    lane = lax.broadcasted_iota(jnp.int32, (128, rows), 0)
    masks = jnp.zeros((128, rows), F32)
    for r in range(routes.shape[0]):
        named = routes[r : r + 1, :]
        masks = jnp.where((lane == named) | (lane == named + experts), 1.0, masks)
    masks = jnp.swapaxes(masks, 0, 1)
    low_lane = lax.broadcasted_iota(jnp.int32, (rows, 128), 1) < experts
    mask = jnp.where(low_lane, masks, 0.0)
    shifted_mask = jnp.where(low_lane, 0.0, masks)
    masked = jnp.where(mask > 0.5, logits, NEG)
    raised = jnp.where(mask > 0.5, jnp.exp(masked - jnp.max(masked, axis=1, keepdims=True)), 0.0)
    probs = raised / jnp.sum(raised, axis=1, keepdims=True)
    gates[...] = probs
    ext[:, pl.ds(width, 128)] = (probs + shifted_mask).astype(BF16)
    for ring in (ring_u, ring_d):
        ring.step(4)
    own[7].wait()
    for i in (7, 8, 9):
        swaps[i].wait_recv()
    for ring in (ring_u, ring_d, ring_c):
        ring.end()
    for ring in (ring_w, ring_o, ring_kv, ring_u, ring_d, ring_c):
        ring.flush()
    for copy in swaps:
        copy.wait_send()
    swap_mixed.wait_send()
    for copy in stores:
        copy.wait()


def front_fused(
    tokens, cotangent, piece_order, seq_lengths, routes, w_query, w_key, w_value, w_router, gain_one, gain_two, w_out,
    shared_up, shared_down, expert_up, expert_down, blks, collective_id,
):
    chips, half = blks // 2, blks // 4
    rows, width = tokens.shape
    dense = w_query.shape[0]
    qw, kw, sw = w_query.shape[1] // 2, w_key.shape[1] // 2, shared_up.shape[1] // 4
    groups, repeats = kw // HD, qw // kw
    dma = pltpu.SemaphoreType.DMA
    vmem = pl.BlockSpec(memory_space=pltpu.VMEM)
    anywhere = pl.BlockSpec(memory_space=pl.ANY)
    smem = pl.BlockSpec(memory_space=pltpu.SMEM)
    out = [
        ((2 * rows, width), BF16, anywhere), ((2 * rows, qw), BF16, anywhere), ((2 * blks, rows, 2 * kw), BF16, anywhere),
        ((2, blks, dense, qw + 2 * kw + 128), BF16, anywhere), ((blks, w_out.shape[0], width), BF16, anywhere),
        ((2, blks, dense, 2 * sw), BF16, anywhere), ((blks, shared_down.shape[0], width), BF16, anywhere),
        ((blks, rows, width), BF16, anywhere), ((2, rows, width), BF16, anywhere),
        (expert_up.shape, BF16, anywhere), (expert_down.shape, BF16, anywhere),
        ((2 * rows, qw), BF16, anywhere), ((2 * rows, qw), F32, anywhere), ((groups, 2, repeats * PIECE), F32, vmem),
        ((rows, width), F32, vmem), ((rows, width + 128), BF16, vmem), ((rows, 128), F32, vmem), ((blks + 8, width), F32, vmem),
        ((2 * blks,), jnp.int32, smem),
    ]
    ring = [dma((12, half + 1))] * 4 + [dma((12, 2 * half + 1))] * 2
    (
        n1, query, kv, first_w, out_w, up_w, down_w, cot, cot_pair, expert_in, expert_out,
        low, full, lse, resid, ext, gates, turned, slots,
    ) = pl.pallas_call(
        functools.partial(front_kernel, chips, blks),
        out_shape=[jax.ShapeDtypeStruct(s, t) for s, t, _ in out],
        in_specs=[smem] * 2 + [vmem] * 4 + [anywhere, vmem] + [anywhere] * 4 + [vmem] * 2 + [anywhere] * 2,
        out_specs=[space for _, _, space in out],
        scratch_shapes=[pltpu.VMEM((dense, 128), BF16)] + [pltpu.VMEM(out[i][0], out[i][1]) for i in (0, 1, 2, 3, 4, 11, 12)] + [
            pltpu.VMEM((128, width), F32), pltpu.VMEM((2, rows, width), BF16), pltpu.VMEM((rows, width), BF16), pltpu.VMEM((rows, width), BF16)]
        + ring + [dma((11,)), dma((11,)), dma((11,)), dma((7,))],
        compiler_params=pltpu.CompilerParams(
            collective_id=collective_id, has_side_effects=True, vmem_limit_bytes=56 << 20),
    )(
        piece_order, seq_lengths, routes.T, w_router.T, gain_one[None], gain_two[None], tokens, cotangent,
        w_query, w_key, w_value, w_out, shared_up, shared_down, expert_up, expert_down)
    return (
        n1, query, kv, first_w.reshape(width, -1)[:, : qw + 2 * kw], out_w.reshape(-1, width),
        up_w.reshape(width, -1), down_w.reshape(-1, width), cot, cot_pair.reshape(2 * rows, width),
        expert_in, expert_out, low, full, lse, resid, ext, gates,
        None, None, None, (first_w, turned, slots))


class Scatter:
    def __init__(self, info, chips, chunks, first, sems):
        self.core, self.at, self.sib = info
        self.half = chips // 2
        self.chunks, self.first = chunks, first
        self.ex_s, self.ex_r, self.right_s, self.right_r, self.left_s, self.left_r = sems
        self.there, self.sent = set(), []

    def remote(self, src, dst, ssem, rsem, dev):
        return pltpu.make_async_remote_copy(
            src_ref=src, dst_ref=dst, send_sem=ssem, recv_sem=rsem,
            device_id={"blk": dev}, device_id_type=MESH)

    def over(self, c, d):
        own, other = self.chunks[c][:2]
        i, k = self.first + c, d + self.half
        place = self.at(d)
        return self.remote(
            own(place + 1 - 2 * self.core), other.at[lax.div(place, 2)], self.ex_s.at[i, k], self.ex_r.at[i, k], self.sib)

    def exchange(self):
        for d in sorted(range(1 - self.half, self.half + 1), key=lambda d: (-abs(d), -d)):
            for c in range(len(self.chunks)):
                copy = self.over(c, d)
                copy.start()
                self.sent.append(copy)

    def join(self, c, d, into, received):
        own, other = self.chunks[c][:2]
        if (c, d) not in self.there:
            self.there.add((c, d))
            self.over(c, d).wait_recv()
        place = self.at(d)
        mine, theirs = own(place), other.at[lax.div(place, 2)]
        rows = mine.shape[0]

        @pl.loop(0, rows // 16)
        def _(i):
            w = pl.ds(pl.multiple_of(i * 16, 16), 16)
            total = mine[w].astype(F32) + theirs[w].astype(F32)
            for ref in received:
                total = total + ref[w].astype(F32)
            into[w] = total.astype(into.dtype)

    def hop(self, c, way, src, s):
        i = self.first + c
        if way > 0:
            return self.remote(
                src, self.chunks[c][2].at[s - 1], self.right_s.at[i, s], self.right_r.at[i, s], self.at(1))
        return self.remote(
            src, self.chunks[c][3].at[s - 1], self.left_s.at[i, s], self.left_r.at[i, s], self.at(-1))

    def hops(self, c, way):
        return self.half - c % 2 if way > 0 else self.half - 1 + c % 2

    def step(self, s):
        for c, (own, _, right, left) in enumerate(self.chunks):
            for way in (1, -1):
                hops = self.hops(c, way)
                if s > hops:
                    continue
                d = way * (hops - s + 1)
                d = self.half if d == -self.half else d
                if s == 1:
                    src = self.chunks[c][1].at[lax.div(self.at(d), 2)]
                    self.join(c, d, src, ())
                else:
                    src = (right if way > 0 else left).at[s - 2]
                    self.hop(c, way, src, s - 1).wait_recv()
                    self.join(c, d, src, (src,))
                copy = self.hop(c, way, src, s)
                copy.start()
                self.sent.append(copy)

    def finish(self, outs):
        for c, (own, _, right, left) in enumerate(self.chunks):
            lasts = []
            for way, buf in ((1, right), (-1, left)):
                hops = self.hops(c, way)
                self.hop(c, way, own(self.at(0)), hops).wait_recv()
                lasts.append(buf.at[hops - 1])
            self.join(c, 0, outs[c], lasts)

    def flush(self):
        for copy in self.sent:
            copy.wait_send()


def tail_kernel(
    chips, experts,
    *refs,
):
    count = 14
    ins, (din,) = refs[:12], refs[12:13]
    input_grad, query_grad, key_grad, value_grad, out_grad, up_grad, down_grad, small_grad, other_up = refs[13:22]
    held = refs[22:34]
    dk, dv, dq, n1, first_w, tokens, hidden_grad, turned, out_part, up_part, down_part, row_part = held
    (
        kv_sum, qkv_part, qkv_sum, up_sum, small_part, small_sum, to_other, from_other, qkv_from, up_from, small_from,
    ) = refs[34:45]
    rest = refs[45:]
    h = lax.axis_index("head")
    blk, core, at, sib = ring_info(chips)
    half = chips // 2
    rows, width = tokens.shape
    qw, kw = dq.shape[1], dk.shape[2]
    top = qw + 2 * kw
    dense = first_w.shape[2]
    sw = up_part.shape[3] // 2
    others, rights, lefts = rest[:count], rest[count : 2 * count], rest[2 * count : 3 * count]
    sems, (y_send, y_recv, load_sem) = rest[3 * count : 3 * count + 6], rest[3 * count + 6 :]
    loads = [pltpu.make_async_copy(a, b, load_sem.at[i]) for i, (a, b) in enumerate(zip(ins, held))]
    for i in (0, 1, 9, 8, 10, 2, 4, 3, 5, 6, 7, 11):
        loads[i].start()
    barrier = pltpu.get_barrier_semaphore()
    for other in (at(1), at(-1), sib):
        pl.semaphore_signal(barrier, inc=1, device_id={"blk": other}, device_id_type=MESH)
    pl.semaphore_signal(barrier, inc=1, device_id={"head": 1 - h}, device_id_type=MESH)
    pl.semaphore_wait(barrier, 4)

    def cross(i, src, dst):
        return pltpu.make_async_remote_copy(
            src_ref=src, dst_ref=dst, send_sem=y_send.at[i], recv_sem=y_recv.at[i],
            device_id={"head": 1 - h}, device_id_type=MESH)

    info = (core, at, sib)

    def scatter(first, owns):
        chunks = [(own, others[first + i], rights[first + i], lefts[first + i]) for i, own in enumerate(owns)]
        return Scatter(info, chips, chunks, first, sems)

    def pieces_at(ref, i):
        return lambda b: ref.at[2 * b + i]

    def source_at(ref, i):
        return lambda b: ref.at[i, b]

    def rows_at(ref, start, size):
        return lambda b: ref.at[b, pl.ds(start, size)]

    out_rows, down_rows = out_part.shape[1], down_part.shape[1]
    kv_ring = scatter(0, [pieces_at(dk, 0), pieces_at(dk, 1), pieces_at(dv, 0), pieces_at(dv, 1)])
    rest_ring = scatter(4, [
        source_at(up_part, 0), source_at(up_part, 1), rows_at(out_part, 0, 32), rows_at(out_part, 32, out_rows - 32),
        rows_at(down_part, 0, down_rows // 2), rows_at(down_part, down_rows // 2, down_rows // 2)])
    qkv_ring = scatter(10, [source_at(qkv_part, 0), source_at(qkv_part, 1)])
    small_ring = scatter(12, [source_at(small_part, 0), source_at(small_part, 1)])

    loads[0].wait()
    loads[1].wait()
    kv_ring.exchange()
    size = width // 2
    swap_up = cross(0, din.at[pl.ds(pl.multiple_of((1 - h) * size, 128), size)], other_up)
    swap_up.start()
    for i in (8, 9, 10):
        loads[i].wait()
    rest_ring.exchange()
    for s in range(1, half + 1):
        kv_ring.step(s)
        if s % 2 == 0:
            rest_ring.step(s // 2)
    kv_ring.finish([kv_sum.at[i, pl.ds(j * rows, rows)] for i in range(2) for j in range(2)])

    for i in (2, 3, 4, 5, 6, 7, 11):
        loads[i].wait()
    theirs = pl.ds(pl.multiple_of((1 - h) * rows, rows), rows)
    ours = pl.ds(pl.multiple_of(h * rows, rows), rows)
    step = 8 * dense

    def norm_grad(where, i, t):
        def part(a, first, n):
            return dot_last(a, first_w[i, pl.ds(t * 8, 8), :, pl.ds(first, n)].reshape(step, n))

        return part(dq[where, :], 0, qw) + part(kv_sum[0, where, :], qw, kw) + part(kv_sum[1, where, :], qw + kw, kw)

    spans = [(i, t, pl.ds(i * (width // 2) + t * step, step)) for i in range(2) for t in range(width // (2 * step))]
    for i, t, c in spans:
        to_other[:, c] = norm_grad(theirs, i, t).astype(BF16)
    swap_norm = cross(1, to_other, from_other)
    swap_norm.start()
    for i, t, c in spans:
        lhs = n1[:, c]
        for first, n, rhs in ((0, qw, dq[...]), (qw, kw, kv_sum[0]), (qw + kw, kw, kv_sum[1])):
            part = dot_first(lhs, rhs).astype(BF16)
            qkv_part[i, pl.ds(t * 8, 8), :, pl.ds(first, n)] = part.reshape(8, dense, n)
    qkv_ring.exchange()
    rest_ring.step(3)
    qkv_ring.step(1)
    for i, t, c in spans:
        input_grad[:, c] = norm_grad(ours, i, t)
    swap_norm.wait_recv()
    rest_ring.step(4)
    qkv_ring.step(2)

    def norm_rows(n, total):
        part = pl.ds(pl.multiple_of(n * 32, 32), 32)
        x = tokens[part, :].astype(F32)
        up = input_grad[part, :] + from_other[part, :].astype(F32)
        scaler = lax.rsqrt(jnp.mean(x * x, axis=1, keepdims=True) + EPS)
        normed = x * scaler
        scaled = up * turned[pl.ds(experts, 1), :]
        back = scaler * (scaled - normed * jnp.mean(scaled * normed, axis=1, keepdims=True))
        input_grad[part, :] = hidden_grad[part, :] + back
        return total + jnp.sum(up * normed, axis=0, keepdims=True)

    gain = lax.fori_loop(0, rows // 32, norm_rows, jnp.zeros((1, width), F32))
    ids = lax.broadcasted_iota(jnp.int32, (128, 1), 0)
    turned_part = jnp.swapaxes(row_part[...] + jnp.where(ids == experts, gain, 0.0), 0, 1)
    small_part[...] = turned_part.astype(BF16).reshape(small_part.shape)
    small_ring.exchange()
    small_ring.step(1)
    qkv_ring.step(3)
    small_ring.step(2)
    up_views = [up_sum.at[0], up_sum.at[1]]
    rest_ring.finish(up_views + [
        out_grad.at[pl.ds(0, 32)], out_grad.at[pl.ds(32, out_rows - 32)],
        down_grad.at[pl.ds(0, down_rows // 2)], down_grad.at[pl.ds(down_rows // 2, down_rows // 2)]])
    swap_sum = cross(2, up_sum.at[1 - h], up_from)
    swap_sum.start()
    qkv_ring.step(4)
    small_ring.step(3)
    qkv_ring.finish([qkv_sum.at[0], qkv_sum.at[1]])
    swap_qkv = cross(3, qkv_sum.at[1 - h], qkv_from)
    swap_qkv.start()
    small_ring.step(4)
    small_ring.finish([small_sum.at[0], small_sum.at[1]])
    swap_small = cross(4, small_sum.at[1 - h], small_from)
    swap_small.start()

    def place(ref, source, first, n, base=0):
        for who, part in ((h, source[0]), (1 - h, source[1])):
            ref[:, pl.ds(pl.multiple_of(base + who * n, 128), n)] = part[:, pl.ds(first, n)].astype(F32)

    swap_sum.wait_recv()
    ups = (up_sum.at[h], up_from)
    place(up_grad, ups, 0, sw)
    place(up_grad, ups, sw, sw, 2 * sw)
    swap_qkv.wait_recv()
    sums = (qkv_sum.at[h], qkv_from)
    place(query_grad, sums, 0, qw)
    place(key_grad, sums, qw, kw)
    place(value_grad, sums, qw + kw, kw)
    swap_small.wait_recv()
    small_grad[...] = small_sum[h] + small_from[...]
    for ring in (kv_ring, rest_ring, qkv_ring, small_ring):
        ring.flush()
    for copy in (swap_norm, swap_up, swap_sum, swap_qkv, swap_small):
        copy.wait_send()
    swap_up.wait_recv()


def tail_fused(
    dk, dv, dq, n1, first_w, tokens, hidden_grad, turned, out_part, up_part, down_part, row_part, din,
    blks, collective_id,
):
    chips, half = blks // 2, blks // 4
    rows, width = tokens.shape
    qw, kw = dq.shape[1], dk.shape[2]
    top = qw + 2 * kw
    dense = first_w.shape[2]
    out_rows, down_rows, up_wide = out_part.shape[1], down_part.shape[1], up_part.shape[3]
    dma = pltpu.SemaphoreType.DMA
    vmem = pl.BlockSpec(memory_space=pltpu.VMEM)
    anywhere = pl.BlockSpec(memory_space=pl.ANY)
    shapes = [(rows, kw)] * 4 + [(dense, up_wide)] * 2 + [(32, width), (out_rows - 32, width)]
    shapes += [(down_rows // 2, width)] * 2 + [(dense, top)] * 2 + [(dense, 128)] * 2
    others = [pltpu.VMEM((chips,) + s, BF16) for s in shapes]
    slots = [pltpu.VMEM((half,) + s, BF16) for s in shapes]
    n = len(shapes)
    held = (dk, dv, dq, n1, first_w, tokens, hidden_grad, turned, out_part, up_part, down_part, row_part)

    def f32(*shape):
        return jax.ShapeDtypeStruct(shape, F32)

    def low(*shape):
        return pltpu.VMEM(shape, BF16)

    return pl.pallas_call(
        functools.partial(tail_kernel, chips, blks),
        out_shape=[
            f32(rows, width), f32(dense, 2 * qw), f32(dense, 2 * kw), f32(dense, 2 * kw), f32(out_rows, width),
            f32(dense, 2 * up_wide), f32(down_rows, width), f32(dense, 128),
            jax.ShapeDtypeStruct((din.shape[0] // 2, din.shape[1]), BF16),
        ],
        in_specs=[anywhere] * 13,
        out_specs=[vmem] * 8 + [anywhere],
        scratch_shapes=[pltpu.VMEM(a.shape, a.dtype) for a in held] + [
            low(2, 2 * rows, kw), low(2, blks, dense, top), low(2, dense, top), low(2, dense, up_wide),
            low(2, blks, dense, 128), pltpu.VMEM((2, dense, 128), F32), low(rows, width), low(rows, width),
            low(dense, top), low(dense, up_wide), pltpu.VMEM((dense, 128), F32),
        ] + others + slots + slots + [dma((n, 2 * half + 1))] * 2 + [dma((n, half + 1))] * 4 + [dma((5,)), dma((5,)), dma((12,))],
        compiler_params=pltpu.CompilerParams(
            collective_id=collective_id, has_side_effects=True, vmem_limit_bytes=62 << 20),
    )(*held, din)


def experts_plain(own_ext, weights, cot_all, blks, capacity, collective_id):
    h, b = lax.axis_index("head"), lax.axis_index("blk")
    own_up, other_up, own_down, other_down = weights
    expert_in = pair(own_up, other_up).reshape(2 * own_up.shape[0], -1)
    expert_out = jnp.where(
        h == 0,
        jnp.concatenate([own_down, other_down], axis=1),
        jnp.concatenate([other_down, own_down], axis=1),
    )
    normed = own_ext[:, : expert_in.shape[0]]
    normed_pair = pair(normed, swap(normed))
    experts, width = blks, expert_in.shape[0]
    rows = own_ext.shape[0]
    ext = all_gather_blk([own_ext], blks, collective_id)[0]
    norm_all = ext[:, :, :width]
    gate_here = lax.dynamic_index_in_dim(ext, width + b, 2, keepdims=False).astype(F32)
    mask_here = lax.dynamic_index_in_dim(ext, width + experts + b, 2, keepdims=False).astype(F32)
    rank = jnp.cumsum(mask_here, axis=1) - mask_here
    slots = jnp.arange(capacity, dtype=F32)
    deal = ((rank[:, None, :] == slots[None, :, None]) & (mask_here[:, None, :] > 0)).astype(BF16)
    deal_gate = deal * gate_here[:, None, :].astype(BF16)

    def to_slots(dealer, array):
        moved = jnp.einsum("bst,btd->bsd", dealer, array, preferred_element_type=F32)
        return moved.astype(BF16).reshape(blks * capacity, width)

    def to_rows(dealer, array):
        return jnp.einsum(
            "bst,bsd->btd", dealer, array.reshape(blks, capacity, width), preferred_element_type=F32)

    expert_rows = to_slots(deal, norm_all)
    both = dot(expert_rows, expert_in)
    ew = expert_out.shape[0]
    gate_part, up_part = both[:, :ew], both[:, ew:]
    activated = (jax.nn.silu(gate_part) * up_part).astype(BF16)
    result = dot(activated, expert_out).astype(BF16)
    result_rows = to_rows(deal, result)
    gate_grad = jnp.sum(result_rows * cot_all.astype(F32), axis=2, keepdims=True)
    routed = (result_rows * gate_here[:, :, None]).astype(BF16)
    slot_grad = to_slots(deal_gate, cot_all)
    act_grad = dot_last(slot_grad, expert_out)
    both_grad = gated_grad(act_grad, gate_part, up_part)
    rows_back = to_rows(deal, dot_last(both_grad, expert_in).astype(BF16)).astype(BF16)
    lane = jnp.arange(128 * (-(-2 * experts // 128)), dtype=jnp.int32)
    grad_high = gate_grad.astype(BF16)
    grad_low = (gate_grad - grad_high.astype(F32)).astype(BF16)
    grad_lanes = jnp.where(lane == b, grad_high, jnp.where(lane == b + experts, grad_low, jnp.zeros((), BF16)))
    dwn = dot_first(activated, slot_grad).astype(BF16)
    dup = dot_first(expert_rows, both_grad).astype(BF16)
    home = reduce_scatter_blk([jnp.concatenate([rows_back, grad_lanes], axis=2)], blks, collective_id + 1, [F32])[0]
    routed_sum = reduce_scatter_blk([routed], blks, collective_id + 2, [F32])[0]
    return home, routed_sum, dup, dwn, normed_pair


def pair(own, other):
    return jnp.where(lax.axis_index("head") == 0, jnp.stack([own, other]), jnp.stack([other, own]))


def half(w, i, parts=1):
    size = w.shape[1] // (2 * parts)
    cut = lax.dynamic_slice_in_dim(w.reshape(w.shape[0], parts, 2 * size), i * size, size, 2)
    return cut.reshape(w.shape[0], parts * size)


def pick(stacked, i):
    return lax.dynamic_index_in_dim(stacked, i, 0, keepdims=False)


def front_plain(
    tokens, cotangent, where, mask, w_query, w_key, w_value, small, w_out, shared_up, shared_down,
    expert_up, expert_down, blks, collective_id,
):
    h = lax.axis_index("head")
    rows, width = tokens.shape
    experts = blks

    def columns(i):
        return jnp.concatenate([half(w_query, i), half(w_key, i), half(w_value, i)], axis=1)

    first = pair(
        jnp.concatenate([columns(h), small], axis=1),
        swap(jnp.concatenate([columns(1 - h), small], axis=1)),
    )
    tokens_pair = pair(tokens, swap(tokens))
    cotangent_pair = pair(cotangent, swap(cotangent)).reshape(2 * rows, width)
    up_pair = pair(half(shared_up, h, 2), swap(half(shared_up, 1 - h, 2)))
    other_up, other_down = swap(expert_up), swap(expert_down)
    gathered = all_gather_blk([first], blks, collective_id)[0].reshape(width, -1)
    qw = w_query.shape[1] // 2
    kw = w_key.shape[1] // 2
    full_qkv = gathered[:, : qw + 2 * kw]
    full_router = gathered[:, qw + 2 * kw : qw + 2 * kw + experts]
    gain_first = gathered[:, qw + 2 * kw + experts].astype(F32)
    gain_second = gathered[:, qw + 2 * kw + experts + 1].astype(F32)

    inputs_pair = tokens_pair.reshape(2 * rows, width).astype(F32)
    normed_one = (inputs_pair * inv_scale(inputs_pair) * gain_first).astype(BF16)
    qkv = dot(normed_one, full_qkv).astype(BF16)
    query = qkv[:, :qw]
    kv = all_gather_blk([qkv[:, qw:]], blks, collective_id + 1)[0].reshape(-1, PIECE, 2 * kw)

    attended, attended_full, lse = attention_forward(query, kv, where)

    up_all, out_all, down_all, cot_all = all_gather_blk([up_pair, w_out, shared_down, cotangent], blks, collective_id + 2)
    full_up = up_all.reshape(width, -1)
    full_out = out_all.reshape(-1, width)
    full_down = down_all.reshape(-1, width)

    mixed = dot(attended, full_out).reshape(2, rows, width)
    inputs = tokens.astype(F32)
    resid = inputs + (pick(mixed, h) + swap(pick(mixed, 1 - h).astype(BF16)).astype(F32))
    scaler_two = inv_scale(resid)
    normed_two = (resid * scaler_two * gain_second).astype(BF16)

    logits = dot(normed_two, full_router)
    masked = jnp.where(mask, logits, NEG)
    raised = jnp.where(mask, jnp.exp(masked - jnp.max(masked, axis=1, keepdims=True)), 0.0)
    gates = raised / jnp.sum(raised, axis=1, keepdims=True)
    extra = jnp.concatenate(
        [gates.astype(BF16), mask.astype(BF16), jnp.zeros((rows, -2 * experts % 128), BF16)], axis=1)
    ext = jnp.concatenate([normed_two, extra], axis=1)
    return (
        normed_one, query, kv, full_qkv, full_out, full_up, full_down, cot_all, cotangent_pair, other_up, other_down,
        attended, attended_full, lse, resid, ext, gates, full_router.T, gain_first, gain_second, None)


def finish_kernel(experts, count, h_ref, up_own, up_other, down_own, down_other, small, *refs):
    up_out, down_out, router_out, one_out, two_out = refs[count : count + 5]
    up_out[...] = up_own[...].astype(F32) + up_other[...].astype(F32)
    down_out[...] = down_own[...].astype(F32) + down_other[...].astype(F32)

    @pl.when(pl.program_id(0) == 0)
    def _():
        for source, target in zip(refs[:count], refs[count + 5 :]):
            target[...] = source[...]
        turned = jnp.swapaxes(small[...], 0, 1)
        router_out[...] = turned[:experts]
        one_out[...] = turned[experts : experts + 1]
        two_out[...] = turned[experts + 1 : experts + 2]


def finish_fused(h, dup, add_up, dwn, add_down, small, experts, others):
    steps = 4
    up_rows, down_rows = add_up.shape[0] // steps, add_down.shape[0] // steps
    up = pl.BlockSpec((up_rows, add_up.shape[1]), lambda i, *_: (i, 0))
    down = pl.BlockSpec((down_rows, add_down.shape[1]), lambda i, *_: (i, 0))
    dense = small.shape[0]
    made = [(add_up.shape, F32), (add_down.shape, F32), ((experts, dense), F32), ((1, dense), F32), ((1, dense), F32)]

    def still(shape):
        return pl.BlockSpec(shape, lambda i, *_: (0, 0))

    rest = [still(a.shape) for a in others]
    return pl.pallas_call(
        functools.partial(finish_kernel, experts, len(others)),
        grid_spec=pltpu.PrefetchScalarGridSpec(
            num_scalar_prefetch=1,
            grid=(steps,),
            in_specs=[
                pl.BlockSpec((up_rows, add_up.shape[1]), lambda i, h: (h[0] * steps + i, 0)), up,
                pl.BlockSpec((down_rows, add_down.shape[1]), lambda i, h: (i, h[0])), down,
                still(small.shape),
            ] + rest,
            out_specs=[up, down] + [still(s) for s, _ in made[2:]] + rest,
        ),
        out_shape=[jax.ShapeDtypeStruct(s, t) for s, t in made + [(a.shape, a.dtype) for a in others]],
        compiler_params=pltpu.CompilerParams(vmem_limit_bytes=63 << 20),
    )(h.reshape(1), dup, add_up, dwn, add_down, small, *others)


def shards(
    tokens, cotangent, seq_lengths, piece_order, routes, norm1_gain, w_query, w_key, w_value, w_out,
    norm2_gain, w_router, shared_up, shared_down, expert_up, expert_down,
):
    blks = lax.axis_size("blk")
    h, b = lax.axis_index("head"), lax.axis_index("blk")
    rows, width = tokens.shape
    experts = blks
    capacity = rows * TOP * 4 // (3 * blks)
    dense_rows = w_query.shape[0]

    fits = blks == 16 and rows == 128 and 2 * capacity == 128 and width % 768 == 0 and dense_rows == 48
    if fits:
        got = front_fused(
            tokens, cotangent, piece_order, seq_lengths, routes, w_query, w_key, w_value, w_router, norm1_gain,
            norm2_gain, w_out, shared_up, shared_down, expert_up[0], expert_down[0], blks, 0)
        slots = got[-1][2]
    else:
        small = jnp.concatenate(
            [w_router, norm1_gain[:, None], norm2_gain[:, None],
             jnp.zeros((dense_rows, -(experts + 2) % 128), BF16)], axis=1)
        lanes = small.shape[1]
        places = jnp.swapaxes(piece_order.reshape(2, blks), 0, 1).reshape(-1)
        order = jnp.arange(2 * blks, dtype=jnp.int32)
        slots = jnp.sum(jnp.where(places[None, :] == order[:, None], order[None, :], 0), axis=1)
    own_places = lax.dynamic_slice_in_dim(piece_order.reshape(2, blks), b, 1, 1).reshape(2)
    where = (slots, own_places, seq_lengths)
    if not fits:
        hot = routes[:, :, None] == jnp.arange(experts, dtype=jnp.int32)[None, None, :]
        mask = jnp.any(hot, axis=1)
        got = front_plain(
            tokens, cotangent, where, mask, w_query, w_key, w_value, small, w_out, shared_up, shared_down,
            expert_up[0], expert_down[0], blks, 0)
    (
        normed_one, query, kv, full_qkv, full_out, full_up, full_down, cot_all, cotangent_pair, other_up, other_down,
        attended, attended_full, lse, resid, ext, gates, router_rows, gain_first, gain_second, kept,
    ) = got
    qw, kw = w_query.shape[1] // 2, w_key.shape[1] // 2
    shared_width = full_down.shape[0]
    inputs = tokens.astype(F32)
    if fits:
        (
            output, hidden_grad, mixed_grad, out_part, shared_up_part, shared_down_part, dup, dwn, row_part, _, add_down,
        ) = experts_fused(
            ext, (expert_up[0], other_up, expert_down[0], other_down), cot_all, (full_up, full_down), cotangent_pair,
            cotangent, resid, gates, kept[1], attended, full_out, blks, capacity, 3)
        query_grad, *kv_parts = attention_backward(query, kv, attended_full, lse, mixed_grad, where)
        (
            input_grad, w_query_grad, w_key_grad, w_value_grad, out_sum, up_grad, down_sum, small_sum, add_up,
        ) = tail_fused(
            *kv_parts, query_grad, normed_one, kept[0], tokens, hidden_grad, kept[1],
            out_part.reshape(blks, dense_rows, width),
            shared_up_part.reshape(2, blks, dense_rows, -1),
            shared_down_part.reshape(blks, -1, width), row_part, dup, blks, 6)
        (
            expert_up_grad, expert_down_grad, router_grad, gain_one_grad, gain_two_grad, output,
            input_grad, w_query_grad, w_key_grad, w_value_grad, out_sum, up_grad, down_sum,
        ) = finish_fused(
            h, dup, add_up, dwn, add_down, small_sum, experts,
            (output, input_grad, w_query_grad, w_key_grad, w_value_grad, out_sum, up_grad, down_sum))
        return (
            output, input_grad, gain_one_grad.reshape(-1), w_query_grad, w_key_grad, w_value_grad,
            out_sum, gain_two_grad.reshape(-1), router_grad.T, up_grad, down_sum,
            expert_up_grad[None], expert_down_grad[None],
        )
    scaler_two = inv_scale(resid)
    normed_two = ext[:, :width]

    home, routed_sum, dup, dwn, normed_pair = experts_plain(
        ext, (expert_up[0], other_up, expert_down[0], other_down), cot_all, blks, capacity, 3)
    normed_pair = normed_pair.reshape(2 * rows, width)
    shared_both = dot(normed_pair, full_up)
    shared_gate, shared_lift = shared_both[:, :shared_width], shared_both[:, shared_width:]
    shared_act = (jax.nn.silu(shared_gate) * shared_lift).astype(BF16)
    shared_sum = dot(shared_act, full_down).reshape(2, rows, width)
    shared_down_part = dot_first(shared_act, cotangent_pair)
    shared_grad = gated_grad(dot_last(cotangent_pair, full_down), shared_gate, shared_lift)
    shared_up_part = dot_first(normed_pair, shared_grad)
    shared_back = dot_last(shared_grad, full_up).reshape(2, rows, width)
    output = (
        resid + routed_sum + pick(shared_sum, h) + swap(pick(shared_sum, 1 - h).astype(BF16)).astype(F32)
    ).astype(BF16)

    dgate = home[:, width : width + experts] + home[:, width + experts : width + 2 * experts]
    weighted = gates * dgate
    logit_grad = (weighted - gates * jnp.sum(weighted, axis=1, keepdims=True)).astype(BF16)
    norm_two_grad = (
        home[:, :width] + dot(logit_grad, router_rows)
        + pick(shared_back, h) + swap(pick(shared_back, 1 - h).astype(BF16)).astype(F32)
    )
    back, gain_two_part = norm_back(resid, scaler_two, gain_second, norm_two_grad)
    hidden_grad = cotangent.astype(F32) + back
    hidden_low = hidden_grad.astype(BF16)
    hidden_pair = pair(hidden_low, swap(hidden_low)).reshape(2 * rows, width)
    out_part = dot_first(attended, hidden_pair)
    mixed_grad = dot_last(hidden_pair, full_out).astype(BF16)
    query_grad, *kv_parts = attention_backward(query, kv, attended_full, lse, mixed_grad, where)
    router_part = dot_first(normed_two, logit_grad)
    dup, dwn, query_grad = lax.optimization_barrier((dup, dwn, query_grad))
    dup = dup.reshape(2, width // 2, -1)
    dwn = jnp.stack([dwn[:, : width // 2], dwn[:, width // 2 :]])
    expert_up_grad = pick(dup, h).astype(F32) + swap(pick(dup, 1 - h)).astype(F32)
    expert_down_grad = pick(dwn, h).astype(F32) + swap(pick(dwn, 1 - h)).astype(F32)
    kv_grads = reduce_scatter_blk([part.reshape(blks, 2 * rows, kw) for part in kv_parts], blks, 6, [BF16] * 2)
    qkv_grad = jnp.concatenate([query_grad, *kv_grads], axis=1)
    norm_one_part = dot_last(qkv_grad, full_qkv).reshape(2, rows, width)
    norm_one_grad = pick(norm_one_part, h) + swap(pick(norm_one_part, 1 - h).astype(BF16)).astype(F32)
    extra_grad, gain_one_part = norm_back(inputs, inv_scale(inputs), gain_first, norm_one_grad)
    input_grad = hidden_grad + extra_grad
    qkv_part = dot_first(normed_one, qkv_grad)
    small_part = jnp.concatenate(
        [router_part, gain_one_part[:, None], gain_two_part[:, None],
         jnp.zeros((width, lanes - experts - 2), F32)], axis=1)

    def by_rows(part):
        return part.astype(BF16).reshape(2, blks, dense_rows, -1)

    qkv_sum, up_sum, out_sum, down_sum, small_sum = reduce_scatter_blk(
        [by_rows(qkv_part), by_rows(shared_up_part),
         out_part.astype(BF16).reshape(blks, dense_rows, width),
         shared_down_part.astype(BF16).reshape(blks, -1, width), by_rows(small_part)],
        blks, 7, [BF16, BF16, F32, F32, F32])
    there = swap(jnp.concatenate([pick(qkv_sum, 1 - h), pick(up_sum, 1 - h)], axis=1)).astype(F32)
    here = jnp.concatenate([pick(qkv_sum, h), pick(up_sum, h)], axis=1).astype(F32)
    small_sum = pick(small_sum, h) + swap(pick(small_sum, 1 - h))

    def whole(start, size):
        return jnp.where(
            h == 0,
            jnp.concatenate([here[:, start : start + size], there[:, start : start + size]], axis=1),
            jnp.concatenate([there[:, start : start + size], here[:, start : start + size]], axis=1))

    top = qw + 2 * kw
    sw = shared_width
    up_grad = jnp.concatenate([whole(top, sw), whole(top + sw, sw)], axis=1)
    return (
        output, input_grad, small_sum[:, experts], whole(0, qw), whole(qw, kw), whole(qw + kw, kw),
        out_sum, small_sum[:, experts + 1], small_sum[:, :experts], up_grad, down_sum,
        expert_up_grad[None], expert_down_grad[None],
    )


def solution(mesh):
    both = P(("head", "blk"), None)
    flat = P(("head", "blk"))
    up, down = P("blk", "head", None), P("blk", None, "head")
    return jax.shard_map(
        shards,
        mesh=mesh,
        in_specs=(both, both, P(), P(), both, flat, both, both, both, both, flat, both, both, both, up, down),
        out_specs=(both, both, flat, both, both, both, both, flat, both, both, both, up, down),
        check_vma=False,
    )
```

profile of v0, /device:TPU:0, one launch (start us, length us, event | category | flops | bytes accessed | tf_op | source)
XLA Modules:
  0.0 369.9 jit_solution(17070832290789487095)
XLA Ops:
  0.6 121.2 %shard_map.255 = (bf16[256,1536]{1,0:T(8,128)(2,1)}, bf16[256,768]{1,0:T(8,128)(2,1)}, bf16[32,128,512]{2,1,0:T(8,128)(2,1)}, bf16[2,16,48,1408]{3,2,1,0:T(8,128...) custom-call(s32[32]{0:T(128)} %order_ref.1, ...), custom_call_target="tpu_custom_call" | custom-call | tf_op jit(solution)/shard_map/pallas_call | solution.py:1390
  121.9 0.0 copy-start
  121.9 128.5 %shard_map.256 = (bf16[128,1536]{1,0:T(8,128)(2,1)}, f32[128,1536]{1,0:T(8,128)}, bf16[256,768]{1,0:T(8,128)(2,1)}, bf16[768,1536]{1,0:T(8,128)(2,1)}, bf16[1536...) custom-call(bf16[128,1664]{1,0:T(8,128)(2,1)} %get-tuple-element.67., ...), custom_call_target="tpu_custom_call" | custom-call | tf_op jit(solution)/shard_map/pallas_call | solution.py:1013
  250.4 0.0 copy-done
  250.4 0.1 reshape.67
  250.5 0.7 dynamic-slice_reduce_fusion.places_ref
  251.2 12.4 %shard_map.257 = (bf16[256,768]{1,0:T(8,128)(2,1)}, bf16[32,128,256]{2,1,0:T(8,128)(2,1)}, bf16[32,128,256]{2,1,0:T(8,128)(2,1)}) custom-call(s32[32]{0:T(128)} %get-tuple-element.80.slots_ref, s32[2]{0:T(128)} %dynamic-slice_reduce_fusion.places_ref, s32[3]{0:T(128)} %lengths_ref.3, bf16[256,768]{1,0:T(8,128)(2,1)} %get-tuple-element.81.q_ref, ...), custom_call_target="tpu_custom_call" | custom-call | tf_op jit(solution)/shard_map/pallas_call | solution.py:463
  263.6 99.1 %shard_map.258 = (f32[128,1536]{1,0:T(8,128)}, f32[48,1536]{1,0:T(8,128)}, f32[48,512]{1,0:T(8,128)}, f32[48,512]{1,0:T(8,128)}, f32[48,1536]{1,0:T(8,128)}, /*i...) custom-call(bf16[32,128,256]{2,1,0:T(8,128)(2,1)} %get-tuple-element.86.refs_0_, ...), custom_call_target="tpu_custom_call" | custom-call | tf_op jit(solution)/shard_map/pallas_call | solution.py:1687
  362.8 6.9 %shard_map.259 = (f32[768,1024]{1,0:T(8,128)}, f32[512,768]{1,0:T(8,128)}, f32[16,48]{1,0:T(8,128)}, f32[1,48]{1,0:T(1,128)}, f32[1,48]{1,0:T(1,128)}, /*index=5...) custom-call(s32[1]{0:T(128)} %bitcast.h_ref, ...), custom_call_target="tpu_custom_call" | custom-call | tf_op jit(solution)/shard_map/pallas_call | solution.py:1859
Async XLA Ops:
  121.9 128.5 %copy-start = (s32[32]{0:T(128)S(1)}, s32[32]{0:T(128)}, u32[]{:S(2)}) copy-start(s32[32]{0:T(128)} %order_ref.1) | copy-start | bytes 388
where the time goes:
time: 375 us; the launch traced here: 370 us
  Pallas kernels  368 us (98%)
    pallas_call x1, Pallas kernels, experts_fused(): pl.pallas_call(functools.partial(expert_kernel, chips, blks), out_shape=[...  128 us
    pallas_call x1, Pallas kernels, front_fused(): pl.pallas_call(functools.partial(front_kernel, chips, blks), out_shape=[j...  121 us
    pallas_call x1, Pallas kernels, tail_fused(): pl.pallas_call(functools.partial(tail_kernel, chips, blks), out_shape=[f3...  99.1 us
    pallas_call x1, Pallas kernels, attention_backward(): pl.pallas_call(functools.partial(backward_kernel, repeats), grid_spec=plt...  12.4 us

commit v1 on v0

--- a/solution.py
+++ b/solution.py
@@ -728,32 +728,6 @@
             exchange_d(g, j).start()
             exchange_o(g, j).start()
 
-    over_right(upper, 0, 0).wait_recv()
-    over_right(lower, 1, 0).wait_recv()
-    cot_copy(1, 0).start()
-    cot_copy(1, 1).start()
-    work(0, 1, 0, None)
-
-    @pl.loop(1, half)
-    def _(g):
-        arrive(g)
-        over_right(upper, 0, g).wait_recv()
-        over_right(lower, 1, g).wait_recv()
-        over_left(lower, 1, g).wait_recv()
-        over_left(upper, 0, g).wait_recv()
-        cot_copy(g + 1, 0).start()
-
-        @pl.when(g < half - 1)
-        def _():
-            cot_copy(g + 1, 1).start()
-
-        work(g, 2, pl.multiple_of(slots + (g - 1) * 2 * slots, slots), g > 1)
-
-    arrive(half)
-    over_right(upper, 0, half).wait_recv()
-    over_left(lower, 1, half).wait_recv()
-    work(half, 1, (2 * half - 1) * slots, True)
-
     arrays = ((0, own_d, sib_d, right_d, left_d, home_ref), (1, own_o, sib_o, right_o, left_o, routed_ref))
     arrived = set()
 
@@ -785,7 +759,7 @@
     )
     sent = []
 
-    def scatter_step(a, s):
+    def scatter_step(a, s, ways=ways):
         _, own, other, to_right, to_left, _ = arrays[a]
         for k, part, way, hops in ways:
             if s > hops:
@@ -805,6 +779,33 @@
             copy.start()
             sent.append(copy)
 
+    over_right(upper, 0, 0).wait_recv()
+    over_right(lower, 1, 0).wait_recv()
+    cot_copy(1, 0).start()
+    cot_copy(1, 1).start()
+    work(0, 1, 0, None)
+
+    @pl.loop(1, half)
+    def _(g):
+        arrive(g)
+        over_right(upper, 0, g).wait_recv()
+        over_right(lower, 1, g).wait_recv()
+        over_left(lower, 1, g).wait_recv()
+        over_left(upper, 0, g).wait_recv()
+        cot_copy(g + 1, 0).start()
+
+        @pl.when(g < half - 1)
+        def _():
+            cot_copy(g + 1, 1).start()
+
+        work(g, 2, pl.multiple_of(slots + (g - 1) * 2 * slots, slots), g > 1)
+
+    arrive(half)
+    over_right(upper, 0, half).wait_recv()
+    over_left(lower, 1, half).wait_recv()
+    scatter_step(0, 1, ways[2:])
+    work(half, 1, (2 * half - 1) * slots, True)
+
     def scatter_finish(a):
         _, own, other, to_right, to_left, into = arrays[a]
         for k, part in ((0, upper), (1, lower)):
@@ -834,7 +835,7 @@
     shared_loads = [
         move(shared_up, in_ref), move(shared_down, out_ref), move(cot_pair, back),
         move(norm_pair.at[0], result.at[pl.ds(0, rows)]), move(norm_pair.at[1], result.at[pl.ds(rows, rows)])]
-    scatter_step(0, 1)
+    scatter_step(0, 1, ways[:2])
 
     def weight_in(c):
         din_ref[c, :] = dot_first(rows_x[:, c], rows_dab[...]).astype(BF16)

time: 375 us -> 371 us (0.989)
    pallas_call x1, Pallas kernels: 12.4 us -> 18.9 us  [attention_backward(): pl.pallas_call(functools.partial(backward_kernel, repeats), grid_spec=plt...]
    pallas_call x1, Pallas kernels: 99.1 us -> 92.8 us  [tail_fused(): pl.pallas_call(functools.partial(tail_kernel, chips, blks), out_shape=[f3...]
where the time goes in v1:
time: 371 us; the launch traced here: 366 us
  Pallas kernels  365 us (98%)
    pallas_call x1, Pallas kernels, experts_fused(): pl.pallas_call(functools.partial(expert_kernel, chips, blks), out_shape=[...  125 us
    pallas_call x1, Pallas kernels, front_fused(): pl.pallas_call(functools.partial(front_kernel, chips, blks), out_shape=[j...  121 us
    pallas_call x1, Pallas kernels, tail_fused(): pl.pallas_call(functools.partial(tail_kernel, chips, blks), out_shape=[f3...  92.8 us
    pallas_call x1, Pallas kernels, attention_backward(): pl.pallas_call(functools.partial(backward_kernel, repeats), grid_spec=plt...  18.9 us

profile of v1, /device:TPU:0, one launch (start us, length us, event | category | flops | bytes accessed | tf_op | source)
XLA Modules:
  0.0 366.5 jit_solution(14294936510076762226)
XLA Ops:
  0.6 121.2 %shard_map.255 = (bf16[256,1536]{1,0:T(8,128)(2,1)}, bf16[256,768]{1,0:T(8,128)(2,1)}, bf16[32,128,512]{2,1,0:T(8,128)(2,1)}, bf16[2,16,48,1408]{3,2,1,0:T(8,128...) custom-call(s32[32]{0:T(128)} %order_ref.1, ...), custom_call_target="tpu_custom_call" | custom-call | tf_op jit(solution)/shard_map/pallas_call | solution.py:1391
  121.9 0.0 copy-start
  121.9 124.9 %shard_map.256 = (bf16[128,1536]{1,0:T(8,128)(2,1)}, f32[128,1536]{1,0:T(8,128)}, bf16[256,768]{1,0:T(8,128)(2,1)}, bf16[768,1536]{1,0:T(8,128)(2,1)}, bf16[1536...) custom-call(bf16[128,1664]{1,0:T(8,128)(2,1)} %get-tuple-element.67., ...), custom_call_target="tpu_custom_call" | custom-call | tf_op jit(solution)/shard_map/pallas_call | solution.py:1014
  246.8 0.0 copy-done
  246.8 0.1 reshape.67
  246.9 0.7 dynamic-slice_reduce_fusion.places_ref
  247.6 18.9 %shard_map.257 = (bf16[256,768]{1,0:T(8,128)(2,1)}, bf16[32,128,256]{2,1,0:T(8,128)(2,1)}, bf16[32,128,256]{2,1,0:T(8,128)(2,1)}) custom-call(s32[32]{0:T(128)} %get-tuple-element.80.slots_ref, s32[2]{0:T(128)} %dynamic-slice_reduce_fusion.places_ref, s32[3]{0:T(128)} %lengths_ref.3, bf16[256,768]{1,0:T(8,128)(2,1)} %get-tuple-element.81.q_ref, ...), custom_call_target="tpu_custom_call" | custom-call | tf_op jit(solution)/shard_map/pallas_call | solution.py:463
  266.5 92.8 %shard_map.258 = (f32[128,1536]{1,0:T(8,128)}, f32[48,1536]{1,0:T(8,128)}, f32[48,512]{1,0:T(8,128)}, f32[48,512]{1,0:T(8,128)}, f32[48,1536]{1,0:T(8,128)}, /*i...) custom-call(bf16[32,128,256]{2,1,0:T(8,128)(2,1)} %get-tuple-element.86.refs_0_, ...), custom_call_target="tpu_custom_call" | custom-call | tf_op jit(solution)/shard_map/pallas_call | solution.py:1688
  359.3 6.9 %shard_map.259 = (f32[768,1024]{1,0:T(8,128)}, f32[512,768]{1,0:T(8,128)}, f32[16,48]{1,0:T(8,128)}, f32[1,48]{1,0:T(1,128)}, f32[1,48]{1,0:T(1,128)}, /*index=5...) custom-call(s32[1]{0:T(128)} %bitcast.h_ref, ...), custom_call_target="tpu_custom_call" | custom-call | tf_op jit(solution)/shard_map/pallas_call | solution.py:1860
Async XLA Ops:
  121.9 125.0 %copy-start = (s32[32]{0:T(128)S(1)}, s32[32]{0:T(128)}, u32[]{:S(2)}) copy-start(s32[32]{0:T(128)} %order_ref.1) | copy-start | bytes 388

commit v2 on v1

--- a/solution.py
+++ b/solution.py
@@ -920,7 +920,7 @@
     tiles(width, 512, norm_part)
 
     def norm_rows(n, total):
-        part = pl.ds(pl.multiple_of(n * 32, 32), 32)
+        part = pl.ds(n * 32, 32)
         x, up = resid[part, :], hidden_grad[part, :]
         scaler = lax.rsqrt(jnp.mean(x * x, axis=1, keepdims=True) + EPS)
         normed = x * scaler
@@ -931,9 +931,13 @@
         hid[h, part, :] = grad.astype(BF16)
         return total + jnp.sum(up * normed, axis=0, keepdims=True)
 
-    gain = lax.fori_loop(0, rows // 32, norm_rows, jnp.zeros((1, width), F32))
-    swap_hid = cross(2, hid.at[h], hid.at[h])
-    swap_hid.start()
+    gain = jnp.zeros((1, width), F32)
+    swap_hid = []
+    for n in range(4):
+        gain = norm_rows(n, gain)
+        block = hid.at[h, pl.ds(n * 32, 32)]
+        swap_hid.append(cross(4 + n, block, block))
+        swap_hid[n].start()
     scatter_step(1, 3)
     row_part[pl.ds(experts + 1, 1), :] = gain
     load_out.wait()
@@ -947,7 +951,8 @@
 
     mixed_tile(h, ours)
     scatter_step(1, 4)
-    swap_hid.wait_recv()
+    for copy in swap_hid:
+        copy.wait_recv()
     mixed_tile(1 - h, theirs)
 
     def out_tile(c):
@@ -966,7 +971,7 @@
             + dot(shared_act[ours, :], out_ref[:, c])).astype(BF16)
 
     tiles(width, 512, output_tile)
-    for copy in (swap_back, swap_sum, swap_hid, swap_down):
+    for copy in (swap_back, swap_sum, swap_down, *swap_hid):
         copy.wait_send()
     swap_down.wait_recv()
     for copy in (up_out, down_out, part_out):
@@ -1029,7 +1034,7 @@
             bf16(half, rows, wide), bf16(half, rows, width), bf16(half, rows, wide), bf16(half, rows, width),
             dma(()), dma((2, 2)),
         ] + [dma((2, half + 1))] * 8 + [dma((2, 2, half + 1))] * 2 + [dma((2, 2, half + 1))] * 4
-        + [dma((4,)), dma((3,)), dma((11,)), dma((4,)), dma((4,))],
+        + [dma((4,)), dma((3,)), dma((11,)), dma((8,)), dma((8,))],
         compiler_params=pltpu.CompilerParams(
             collective_id=collective_id, has_side_effects=True, vmem_limit_bytes=63 << 20),
     )(ext, *weights, cot_all, *shared, cot_pair, cot_own, resid, gates, turned, low, full_out)

time: 371 us -> 371 us (level)
    pallas_call x1, Pallas kernels: 92.8 us -> 101 us  [tail_fused(): pl.pallas_call(functools.partial(tail_kernel, chips, blks), out_shape=[f3...]
    pallas_call x1, Pallas kernels: 18.9 us -> 10.8 us  [attention_backward(): pl.pallas_call(functools.partial(backward_kernel, repeats), grid_spec=plt...]
where the time goes in v2:
time: 371 us; the launch traced here: 367 us
  Pallas kernels  365 us (98%)
    pallas_call x1, Pallas kernels, experts_fused(): pl.pallas_call(functools.partial(expert_kernel, chips, blks), out_shape=[...  125 us
    pallas_call x1, Pallas kernels, front_fused(): pl.pallas_call(functools.partial(front_kernel, chips, blks), out_shape=[j...  121 us
    pallas_call x1, Pallas kernels, tail_fused(): pl.pallas_call(functools.partial(tail_kernel, chips, blks), out_shape=[f3...  101 us
    pallas_call x1, Pallas kernels, attention_backward(): pl.pallas_call(functools.partial(backward_kernel, repeats), grid_spec=plt...  10.8 us

profile of v2, /device:TPU:0, one launch (start us, length us, event | category | flops | bytes accessed | tf_op | source)
XLA Modules:
  0.0 366.7 jit_solution(13466834375291425310)
XLA Ops:
  0.6 121.2 %shard_map.255 = (bf16[256,1536]{1,0:T(8,128)(2,1)}, bf16[256,768]{1,0:T(8,128)(2,1)}, bf16[32,128,512]{2,1,0:T(8,128)(2,1)}, bf16[2,16,48,1408]{3,2,1,0:T(8,128...) custom-call(s32[32]{0:T(128)} %order_ref.1, ...), custom_call_target="tpu_custom_call" | custom-call | tf_op jit(solution)/shard_map/pallas_call | solution.py:1396
  121.9 0.0 copy-start
  121.9 125.0 %shard_map.256 = (bf16[128,1536]{1,0:T(8,128)(2,1)}, f32[128,1536]{1,0:T(8,128)}, bf16[256,768]{1,0:T(8,128)(2,1)}, bf16[768,1536]{1,0:T(8,128)(2,1)}, bf16[1536...) custom-call(bf16[128,1664]{1,0:T(8,128)(2,1)} %get-tuple-element.67., ...), custom_call_target="tpu_custom_call" | custom-call | tf_op jit(solution)/shard_map/pallas_call | solution.py:1019
  246.9 0.0 copy-done
  246.9 0.1 reshape.67
  247.0 0.7 dynamic-slice_reduce_fusion.places_ref
  247.7 10.8 %shard_map.257 = (bf16[256,768]{1,0:T(8,128)(2,1)}, bf16[32,128,256]{2,1,0:T(8,128)(2,1)}, bf16[32,128,256]{2,1,0:T(8,128)(2,1)}) custom-call(s32[32]{0:T(128)} %get-tuple-element.80.slots_ref, s32[2]{0:T(128)} %dynamic-slice_reduce_fusion.places_ref, s32[3]{0:T(128)} %lengths_ref.3, bf16[256,768]{1,0:T(8,128)(2,1)} %get-tuple-element.81.q_ref, ...), custom_call_target="tpu_custom_call" | custom-call | tf_op jit(solution)/shard_map/pallas_call | solution.py:463
  258.5 101.0 %shard_map.258 = (f32[128,1536]{1,0:T(8,128)}, f32[48,1536]{1,0:T(8,128)}, f32[48,512]{1,0:T(8,128)}, f32[48,512]{1,0:T(8,128)}, f32[48,1536]{1,0:T(8,128)}, /*i...) custom-call(bf16[32,128,256]{2,1,0:T(8,128)(2,1)} %get-tuple-element.86.refs_0_, ...), custom_call_target="tpu_custom_call" | custom-call | tf_op jit(solution)/shard_map/pallas_call | solution.py:1693
  359.6 6.9 %shard_map.259 = (f32[768,1024]{1,0:T(8,128)}, f32[512,768]{1,0:T(8,128)}, f32[16,48]{1,0:T(8,128)}, f32[1,48]{1,0:T(1,128)}, f32[1,48]{1,0:T(1,128)}, /*index=5...) custom-call(s32[1]{0:T(128)} %bitcast.h_ref, ...), custom_call_target="tpu_custom_call" | custom-call | tf_op jit(solution)/shard_map/pallas_call | solution.py:1865
Async XLA Ops:
  121.9 125.1 %copy-start = (s32[32]{0:T(128)S(1)}, s32[32]{0:T(128)}, u32[]{:S(2)}) copy-start(s32[32]{0:T(128)} %order_ref.1) | copy-start | bytes 388
